TPU v7x, 128 devices: a whole 4x4x4 slice. The times are simulated.
128 devices in a mesh: ctx: 16 (over x, y_hi, core), exp: 8 (over y_lo, z).
Axes of the slice: x: 4, y: 4 (y_hi: 2, y_lo: 2; y = y_hi * 2 + y_lo), z: 4, core: 2. Of those that a mesh axis runs over, the one named last changes fastest.
Arguments:
- hidden_in: bfloat16 [2048, 4096], P('ctx'), may hold values from -6 to 6
- attn_gain: bfloat16 [4096], replicated, may hold values from 0.099609375 to 1.8984375
- w_query: bfloat16 [4096, 4096], P('ctx', 'exp'), may hold values from -0.1875 to 0.1875
- w_key: bfloat16 [4096, 1024], P('ctx', 'exp'), may hold values from -0.09375 to 0.09375
- w_value: bfloat16 [4096, 1024], P('ctx', 'exp'), may hold values from -0.09375 to 0.09375
- w_out: bfloat16 [4096, 4096], P('exp', 'ctx'), may hold values from -0.375 to 0.375
- prior_keys: bfloat16 [2048, 1024], P('ctx', 'exp'), may hold values from -100 to 100
- prior_values: bfloat16 [2048, 1024], P('ctx', 'exp'), may hold values from -6 to 6
- stretch_offset: int32 [1], replicated, may hold values from 2048 to 30720
- ffn_gain: bfloat16 [4096], replicated, may hold values from 0.099609375 to 1.8984375
- w_gate: bfloat16 [8, 4096, 14336], P('exp', None, 'ctx'), may hold values from -0.09375 to 0.09375
- w_up: bfloat16 [8, 4096, 14336], P('exp', None, 'ctx'), may hold values from -0.09375 to 0.09375
- w_down: bfloat16 [8, 14336, 4096], P('exp', 'ctx'), may hold values from -0.15625 to 0.15625
- expert_ids: int32 [2048, 2], replicated, may hold values from 0 to 7, all different within a row; in each aligned block of 16 rows (0 to 15, 16 to 31, ...) at most 8 rows name the same one
- gate_weights: float32 [2048, 2], P(('ctx', 'exp')), may hold values from 0.1 to 0.9
Outputs:
- output: bfloat16 [2048, 4096], P(('ctx', 'exp'))
Inputs may be any that keep to these rules, and one draw needn't show every extreme that they name: `expert_ids`: each row names two different experts. Within each aligned block of 16 rows no expert is named by more than 8 rows, and in some blocks one expert is named by exactly 8. prior_keys and prior_values belong to positions stretch_offset - 2048 to stretch_offset - 1, in order; prior_keys are already rotated at those positions.
All inputs are finite; a program needn't handle non-finite values.
Results may differ from a plain program's by a relative error of at most 0.03.
The roundings to bfloat16 on the way count: a program that leaves them out, or rounds other values in their place, can miss the bound.
Values may be sent and summed in bfloat16 or wider, within the bound.
A program may use at most 128 MiB of HBM per device.

v0:
```python
import math

import jax
import jax.numpy as jnp
from jax import lax
from jax.sharding import PartitionSpec as P

HEADS = 32
KV_HEADS = 8
HEAD_DIM = 128


def rms_scale(matrix, gain_vec):
    widened = matrix.astype(jnp.float32)
    inverse = lax.rsqrt(jnp.mean(widened * widened, axis=-1, keepdims=True) + 1e-05)
    return (widened * inverse * gain_vec.astype(jnp.float32)).astype(jnp.bfloat16)


def rotate(matrix, positions, head_dim):
    row_count = matrix.shape[0]
    head_count = matrix.shape[1] // head_dim
    half_dim = head_dim // 2
    shaped = matrix.reshape(row_count, head_count, head_dim)
    frequency = jnp.exp(
        jnp.arange(half_dim).astype(jnp.float32) * (-2.0 * math.log(1000000.0) / head_dim)
    )
    angles = positions.astype(jnp.float32)[:, None] * frequency[None, :]
    cosine = jnp.cos(angles)[:, None, :]
    sine_part = jnp.sin(angles)[:, None, :]
    first_half = shaped[:, :, :half_dim]
    second_half = shaped[:, :, half_dim:]
    turned = jnp.concatenate(
        [
            first_half * cosine - second_half * sine_part,
            second_half * cosine + first_half * sine_part,
        ],
        axis=2,
    )
    return turned.reshape(row_count, head_count * head_dim)


def local(
    hidden_in,
    attn_gain,
    w_query,
    w_key,
    w_value,
    w_out,
    prior_keys,
    prior_values,
    stretch_offset,
    ffn_gain,
    w_gate,
    w_up,
    w_down,
    expert_ids,
    gate_weights,
):
    exp_count = lax.axis_size("exp")
    ctx_index = lax.axis_index("ctx")
    exp_index = lax.axis_index("exp")
    local_len = hidden_in.shape[0]
    model_width = hidden_in.shape[1]
    query_width = w_query.shape[1]
    key_width = w_key.shape[1]
    kv_local = key_width // HEAD_DIM
    head_group = HEADS // KV_HEADS
    normed = rms_scale(hidden_in, attn_gain)
    portions = (
        lax.all_gather(w_query, "ctx", axis=0, tiled=True),
        lax.all_gather(w_key, "ctx", axis=0, tiled=True),
        lax.all_gather(w_value, "ctx", axis=0, tiled=True),
    )
    query_raw, key_raw, value_raw = tuple(
        (jnp.dot(normed, portion, preferred_element_type=jnp.float32) for portion in portions)
    )
    positions = stretch_offset[0] + ctx_index * local_len + jnp.arange(local_len, dtype=jnp.int32)
    query_rot = rotate(query_raw, positions, HEAD_DIM).astype(jnp.bfloat16)
    key_now = rotate(key_raw, positions, HEAD_DIM).astype(jnp.bfloat16)
    value_now = value_raw.astype(jnp.bfloat16)
    query_rows = (
        query_rot.reshape(local_len, kv_local, head_group, HEAD_DIM)
        .transpose(1, 0, 2, 3)
        .reshape(kv_local, local_len * head_group, HEAD_DIM)
    )
    query_pos = (
        ctx_index * local_len + jnp.arange(local_len * head_group, dtype=jnp.int32) // head_group
    )
    row_best = jnp.full((kv_local, local_len * head_group), -1e30, jnp.float32)
    prior_k = lax.all_gather(prior_keys, "ctx", axis=0, tiled=True)
    prior_v = lax.all_gather(prior_values, "ctx", axis=0, tiled=True)
    now_k = lax.all_gather(key_now, "ctx", axis=0, tiled=True)
    now_v = lax.all_gather(value_now, "ctx", axis=0, tiled=True)
    key_span = prior_k.shape[0]
    key_index = jnp.arange(key_span, dtype=jnp.int32)
    keys_cat = jnp.concatenate([prior_k, now_k], axis=0).reshape(2 * key_span, kv_local, HEAD_DIM)
    values_cat = jnp.concatenate([prior_v, now_v], axis=0).reshape(2 * key_span, kv_local, HEAD_DIM)
    scores = jnp.einsum(
        "hqd,khd->hqk", query_rows, keys_cat, preferred_element_type=jnp.float32
    ) / math.sqrt(HEAD_DIM)
    visible = jnp.concatenate(
        [key_index[None, :] > query_pos[:, None], key_index[None, :] <= query_pos[:, None]], axis=1
    )[None]
    scores = jnp.where(visible, scores, -1e30)
    new_best = jnp.maximum(row_best, jnp.max(scores, axis=2))
    weights = jnp.where(visible, jnp.exp(scores - new_best[:, :, None]), 0.0)
    row_mass = jnp.sum(weights, axis=2)
    weighted = jnp.einsum(
        "hqk,khd->hqd", weights.astype(jnp.bfloat16), values_cat, preferred_element_type=jnp.float32
    )
    row_best, row_mass, weighted = (new_best, row_mass, weighted)
    blended = weighted / row_mass[:, :, None]
    attended = (
        blended.reshape(kv_local, local_len, head_group, HEAD_DIM)
        .transpose(1, 0, 2, 3)
        .reshape(local_len, query_width)
        .astype(jnp.bfloat16)
    )
    head_part = jnp.dot(
        attended,
        lax.all_gather(w_out, "ctx", axis=1, tiled=True),
        preferred_element_type=jnp.float32,
    )
    summed = lax.psum_scatter(
        head_part.astype(jnp.bfloat16), "exp", scatter_dimension=0, tiled=True
    ).astype(jnp.float32)
    tok_dev = local_len // exp_count
    own_rows = lax.dynamic_slice_in_dim(hidden_in, exp_index * tok_dev, tok_dev, 0)
    residual = (own_rows.astype(jnp.float32) + summed).astype(jnp.bfloat16)
    normed_ffn = rms_scale(residual, ffn_gain)
    capacity = 4 * tok_dev // exp_count
    device_row = (ctx_index * exp_count + exp_index) * tok_dev
    my_ids = lax.dynamic_slice_in_dim(expert_ids, device_row, tok_dev, 0).reshape(-1)
    onehot = (my_ids[:, None] == jnp.arange(exp_count, dtype=jnp.int32)[None, :]).astype(jnp.int32)
    before = jnp.cumsum(onehot, axis=0) - onehot
    slot_of = jnp.sum(before * onehot, axis=1)
    slot_ids = jnp.arange(exp_count * capacity, dtype=jnp.int32)
    select = (
        (slot_ids[:, None] // capacity == my_ids[None, :])
        & (slot_ids[:, None] % capacity == slot_of[None, :])
    ).astype(jnp.bfloat16)
    repeated = jnp.repeat(normed_ffn, 2, axis=0)
    outgoing = (
        jnp.dot(select, repeated, preferred_element_type=jnp.float32)
        .astype(jnp.bfloat16)
        .reshape(exp_count, capacity, model_width)
    )
    arrived = lax.all_to_all(outgoing, "exp", split_axis=0, concat_axis=0, tiled=True)
    gate_mat = w_gate[0]
    up_mat = w_up[0]
    down_mat = w_down[0]
    flattened = lax.all_gather(arrived, "ctx", axis=0, tiled=True).reshape(-1, model_width)
    gate_part = jnp.dot(flattened, gate_mat, preferred_element_type=jnp.float32)
    up_part = jnp.dot(flattened, up_mat, preferred_element_type=jnp.float32)
    hidden_act = (jax.nn.silu(gate_part) * up_part).astype(jnp.bfloat16)
    own_slots = lax.psum_scatter(
        jnp.dot(hidden_act, down_mat, preferred_element_type=jnp.float32).astype(jnp.bfloat16),
        "ctx",
        scatter_dimension=0,
        tiled=True,
    )
    outcome = own_slots.reshape(exp_count, capacity, model_width)
    returned = lax.all_to_all(outcome, "exp", split_axis=0, concat_axis=0, tiled=True)
    gathered_back = jnp.dot(
        select.T,
        returned.reshape(exp_count * capacity, model_width),
        preferred_element_type=jnp.float32,
    )
    picked = gathered_back.reshape(tok_dev, 2, model_width)
    mixture = jnp.sum(gate_weights[:, :, None] * picked, axis=1)
    return (residual.astype(jnp.float32) + mixture).astype(jnp.bfloat16)


def solution(mesh):
    in_specs = (
        P("ctx", None),
        P(),
        P("ctx", "exp"),
        P("ctx", "exp"),
        P("ctx", "exp"),
        P("exp", "ctx"),
        P("ctx", "exp"),
        P("ctx", "exp"),
        P(),
        P(),
        P("exp", None, "ctx"),
        P("exp", None, "ctx"),
        P("exp", "ctx", None),
        P(),
        P(("ctx", "exp"), None),
    )
    out_specs = P(("ctx", "exp"), None)
    return jax.shard_map(local, mesh=mesh, in_specs=in_specs, out_specs=out_specs, check_vma=False)
```

profile of v0, /device:TPU:1, one launch (start us, length us, event | category | flops | bytes accessed | tf_op | source)
XLA Modules:
  0.0 505.1 jit_solution(18308511437357119122)
XLA Ops:
  6.5 0.7 all-gather.9.cloned.1.call-update
  7.3 0.7 all-gather.11.cloned.1.call-update
  9.4 0.7 convert_element_type.89
  10.7 0.9 copy.22
  11.6 1.5 fusion.17
  13.5 28.6 %all_gather.28 = bf16[2048,128]{0,1:T(8,128)(2,1)} all-gather(bf16[128,128]{0,1:T(8,128)(2,1)S(1)} %copy.22), channel_id=1, replica_groups=mesh['ctx'=16,'exp'=8] {'ctx'}, dimensions={0}, use_global_device_ids=true | all-gather | bytes 557056 | tf_op jit(solution)/shard_map/all_gather | solution.py:90
  42.1 22.4 %all_gather.31 = bf16[2048,128]{1,0:T(8,128)(2,1)} all-gather(bf16[128,128]{1,0:T(8,128)(2,1)} %param.22), channel_id=1, replica_groups=mesh['ctx'=16,'exp'=8] {'ctx'}, dimensions={0}, use_global_device_ids=true | all-gather | bytes 557056 | tf_op jit(solution)/shard_map/all_gather | solution.py:91
  64.5 1.3 iota_compare_fusion.1
  65.9 1.8 convolution_bitcast_fusion
  68.0 25.1 %all-gather = bf16[2048,1,128]{0,2,1:T(8,128)(2,1)} all-gather(bf16[128,1,128]{0,2,1:T(8,128)(2,1)S(1)} %pad_maximum_fusion), channel_id=2, replica_groups=mesh['ctx'=16,'exp'=8] {'ctx'}, dimensions={0}, use_global_device_ids=true | all-gather | bytes 557056 | tf_op jit(solution)/shard_map/all_gather | solution.py:92
  93.0 13.0 %all-gather.11.cloned.1.call-done = bf16[4096,128]{1,0:T(8,128)(2,1)} async-done(((bf16[256,128]{1,0:T(8,128)(2,1)}), bf16[4096,128]{1,0:T(8,128)(2,1)}) %all-gather.11.cloned.1.call-update) | async-done | bytes 1048592 | tf_op jit(solution)/shard_map/all_gather | solution.py:72
  106.0 1.7 convolution_convert_fusion.3
  107.7 24.4 %all_gather.33 = bf16[2048,128]{1,0:T(8,128)(2,1)} all-gather(bf16[128,128]{1,0:T(8,128)(2,1)S(1)} %convolution_convert_fusion.3), channel_id=1, replica_groups=mesh['ctx'=16,'exp'=8] {'ctx'}, dimensions={0}, use_global_device_ids=true | all-gather | bytes 557056 | tf_op jit(solution)/shard_map/all_gather | solution.py:93
  132.1 32.0 %all-gather.7.cloned.1.call-done = bf16[4096,512]{1,0:T(8,128)(2,1)} async-done(((bf16[256,512]{1,0:T(8,128)(2,1)}), bf16[4096,512]{1,0:T(8,128)(2,1)}) %all-gather.7.cloned.1.call-update) | async-done | bytes 4194320 | tf_op jit(solution)/shard_map/all_gather | solution.py:70
  164.1 3.6 fusion.76
  167.8 1.0 reshape.280
  169.1 3.4 fusion.4
  172.5 2.8 fusion.8
  175.3 2.3 fusion.24
  177.7 46.4 %all-gather.13.cloned.1.call-done = bf16[512,4096]{1,0:T(8,128)(2,1)} async-done(((bf16[512,256]{1,0:T(8,128)(2,1)}), bf16[512,4096]{1,0:T(8,128)(2,1)}) %all-gather.13.cloned.1.call-update) | async-done | bytes 4194320 | tf_op jit(solution)/shard_map/all_gather | solution.py:121
  224.1 3.9 convolution_convert_fusion.1
  228.9 32.0 %reduce-scatter.3.cloned.1.call-done = bf16[16,4096]{1,0:T(8,128)(2,1)} async-done(((bf16[128,4096]{1,0:T(8,128)(2,1)}), bf16[16,4096]{1,0:T(8,128)(2,1)}) %reduce-scatter.3.cloned.1.call-update) | async-done | bytes 131088 | tf_op jit(solution)/shard_map/reduce_scatter | solution.py:124
  260.8 1.1 fusion.35
  262.7 10.6 %all_to_all.10 = bf16[8,8,4096]{2,1,0:T(8,128)(2,1)} all-to-all(bf16[8,8,4096]{2,1,0:T(8,128)(2,1)S(1)} %fusion.10), channel_id=1, replica_groups=mesh['ctx'=16,'exp'=8] {'exp'}, dimensions={0} | all-to-all | bytes 1048576 | tf_op jit(solution)/shard_map/all_to_all | solution.py:148
  273.3 78.0 %all-gather.15.cloned.1.call-done = bf16[128,8,4096]{2,1,0:T(8,128)(2,1)} async-done(((bf16[8,8,4096]{2,1,0:T(8,128)(2,1)}), bf16[128,8,4096]{2,1,0:T(8,128)(2,1)}) %all-gather.15.cloned.1.call-update) | async-done | bytes 8388624 | tf_op jit(solution)/shard_map/all_gather | solution.py:152
  351.3 12.5 %fusion = f32[1024,896]{1,0:T(8,128)S(1)} fusion(bf16[128,8,4096]{2,1,0:T(8,128)(2,1)} %all-gather.15.cloned.1.call-done, bf16[1,4096,896]{2,1,0:T(8,128)(2,1)} %param.26), kind=kOutput, calls=%fused_computation | convolution fusion | flops 7516192768 | bytes 19398656 | tf_op jit(solution)/shard_map/dot_general | solution.py:154
  363.8 12.1 %multiply_convert_fusion = bf16[1024,896]{1,0:T(8,128)(2,1)S(1)} fusion(f32[1024,896]{1,0:T(8,128)S(1)} %fusion, bf16[1,4096,896]{2,1,0:T(8,128)(2,1)} %param.25, bf16[128,8,4096]{2,1,0:T(8,128)(2,1)S(1)} %copy-done.7), kind=kOutput, calls=%fused_computation.21 | convolution fusion | flops 7521697792 | bytes 21233664 | tf_op jit(solution)/shard_map/dot_general | solution.py:153
  375.9 11.1 %convolution_convert_fusion = bf16[1024,4096]{1,0:T(8,128)(2,1)} fusion(bf16[1024,896]{1,0:T(8,128)(2,1)S(1)} %multiply_convert_fusion, bf16[1,896,4096]{2,1,0:T(8,128)(2,1)S(1)} %bitcast.45), kind=kOutput, calls=%fused_computation.7 | convolution fusion | flops 7520387072 | bytes 17563648 | tf_op jit(solution)/shard_map/dot_general | solution.py:157
  387.0 99.0 %reduce-scatter.5.cloned.1.call-done = bf16[64,4096]{1,0:T(8,128)(2,1)} async-done(((bf16[1024,4096]{1,0:T(8,128)(2,1)}), bf16[64,4096]{1,0:T(8,128)(2,1)}) %reduce-scatter.5.cloned.1.call-update) | async-done | bytes 524304 | tf_op jit(solution)/shard_map/reduce_scatter | solution.py:156
  486.0 4.2 all-to-all-start.1
  490.3 7.0 %all-to-all-done.1 = bf16[8,8,4096]{2,1,0:T(8,128)(2,1)S(1)} async-done(((bf16[8,8,4096]{2,1,0:T(8,128)(2,1)}), bf16[8,8,4096]{2,1,0:T(8,128)(2,1)S(1)}, u32[]{:S(2)}, u32[]{:S(2)}) %all-to-all-start.1) | async-done | bytes 524320 | tf_op jit(solution)/shard_map/all_to_all | solution.py:163
  497.6 0.7 fusion.38
  (60 shorter events, 4.4 us)
Async XLA Ops:
  6.5 221.8 %copy-start = (s32[2048,2]{0,1:T(2,128)S(1)}, s32[2048,2]{0,1:T(2,128)}, u32[]{:S(2)}) copy-start(s32[2048,2]{0,1:T(2,128)} %param.28) | copy-start | bytes 49156
  6.5 59.3 %copy-start.2 = (bf16[128,4096]{1,0:T(8,128)(2,1)S(1)}, bf16[128,4096]{1,0:T(8,128)(2,1)}, u32[]{:S(2)}) copy-start(bf16[128,4096]{1,0:T(8,128)(2,1)} %param.15) | copy-start | bytes 3145732
  6.5 59.3 %all-gather.9.cloned.1.call-start = ((), (), s32[]{:S(2)}) async-start(), calls=%async_computation.5 | async-start | bytes 1114112 | tf_op jit(solution)/shard_map/all_gather | solution.py:71
  7.3 98.8 %all-gather.11.cloned.1.call-start = ((), (), s32[]{:S(2)}) async-start(), calls=%async_computation.6 | async-start | bytes 1114112 | tf_op jit(solution)/shard_map/all_gather | solution.py:72
  8.0 156.1 %all-gather.7.cloned.1.call-start = ((), (), s32[]{:S(2)}) async-start(), calls=%async_computation.4 | async-start | bytes 4456448 | tf_op jit(solution)/shard_map/all_gather | solution.py:70
  8.7 215.4 %all-gather.13.cloned.1.call-start = ((), (), s32[]{:S(2)}) async-start(), calls=%async_computation.7 | async-start | bytes 4456448 | tf_op jit(solution)/shard_map/all_gather | solution.py:121
  9.3 251.5 %reduce-scatter.3.cloned.1.call-start = ((), (), s32[]{:S(2)}) async-start(), calls=%async_computation.8 | async-start | bytes 1179648 | tf_op jit(solution)/shard_map/reduce_scatter | solution.py:124
  172.5 2.8 copy-start.3
  172.5 2.8 copy-start.4
  177.6 50.7 %copy-start.5 = (bf16[4096]{0:T(1024)(128)(2,1)S(1)}, bf16[4096]{0:T(1024)(128)(2,1)}, u32[]{:S(2)}) copy-start(bf16[4096]{0:T(1024)(128)(2,1)} %param.24) | copy-start | bytes 24580
  228.0 123.3 %all-gather.15.cloned.1.call-start = ((), (), s32[]{:S(2)}) async-start(), calls=%async_computation.9 | async-start | bytes 8912896 | tf_op jit(solution)/shard_map/all_gather | solution.py:152
  273.3 212.7 %reduce-scatter.5.cloned.1.call-start = ((), (), s32[]{:S(2)}) async-start(), calls=%async_computation.10 | async-start | bytes 8912896 | tf_op jit(solution)/shard_map/reduce_scatter | solution.py:156
  351.3 12.5 %copy-start.7 = (bf16[128,8,4096]{2,1,0:T(8,128)(2,1)S(1)}, bf16[128,8,4096]{2,1,0:T(8,128)(2,1)}, u32[]{:S(2)}) copy-start(bf16[128,8,4096]{2,1,0:T(8,128)(2,1)} %all-gather.15.cloned.1.call-done) | copy-start | bytes 25165828
  351.3 24.6 %slice-start = ((s8[7340032]{0:T(1024)(128)(4,1)}), s8[4194304]{0:T(1024)(128)(4,1)S(1)}, s32[]{:S(2)}) async-start(s8[7340032]{0:T(1024)(128)(4,1)} %bitcast.44), calls=%async_computation.11 | async-start | bytes 8388608
  363.8 12.1 %slice-start.1 = ((s8[7340032]{0:T(1024)(128)(4,1)}), s8[3145728]{0:T(1024)(128)(4,1)S(1)}, s32[]{:S(2)}) async-start(s8[7340032]{0:T(1024)(128)(4,1)} %bitcast.44), calls=%async_computation.12 | async-start | bytes 6291456
  387.0 111.3 %copy-start.1 = (s32[2048,2]{0,1:T(2,128)S(1)}, s32[2048,2]{0,1:T(2,128)}, u32[]{:S(2)}) copy-start(s32[2048,2]{0,1:T(2,128)} %param.28) | copy-start | bytes 49156
  387.0 110.3 %copy-start.6 = (f32[16,2]{0,1:T(2,128)S(1)}, f32[16,2]{0,1:T(2,128)}, u32[]{:S(2)}) copy-start(f32[16,2]{0,1:T(2,128)} %param.29) | copy-start | bytes 388
  486.0 11.3 %all-to-all-start.1 = ((bf16[8,8,4096]{2,1,0:T(8,128)(2,1)}), bf16[8,8,4096]{2,1,0:T(8,128)(2,1)S(1)}, u32[]{:S(2)}, u32[]{:S(2)}) async-start(bf16[8,8,4096]{2,1,0:T(8,128)(2,1)} %bitcast.41), calls=%async_computation.3 | async-start | bytes 1048576 | tf_op jit(solution)/shard_map/all_to_all | solution.py:163
Sparse Core Ops, SparseCore 0:
  9.8 49.9 all-gather.8
  62.2 43.8 all-gather.10
  108.4 55.6 all-gather.6
  166.2 57.8 all-gather.12
  228.1 32.6 reduce-scatter.2
  273.4 77.8 all-gather.14
  387.1 98.7 reduce-scatter.4
where the time goes:
time: 508 us; the launch traced here: 505 us
  waiting for transfers between devices  310 us (61%)
  blocking collectives  111 us (22%)
  matrix products  53 us (10%)
  between operations  14.4 us (3%)
  other arithmetic  9.39 us (2%)
    reduce_scatter x1, waiting for transfers between devices, local(): lax.psum_scatter(jnp.dot(hidden_act, down_mat, preferred_element_type=jnp...  99 us
    all_gather x1, waiting for transfers between devices, local(): lax.all_gather(arrived, 'ctx', axis=0, tiled=True).reshape(-1, model_width)  78 us
    all_gather x1, waiting for transfers between devices, local(): lax.all_gather(w_out, 'ctx', axis=1, tiled=True)  46.4 us
    all_gather x1, waiting for transfers between devices, local(): lax.all_gather(w_query, 'ctx', axis=0, tiled=True)  32 us
    reduce_scatter x1, waiting for transfers between devices, local(): lax.psum_scatter(head_part.astype(jnp.bfloat16), 'exp', scatter_dimension...  32 us
    all_gather x1, blocking collectives, local(): prior_k = lax.all_gather(prior_keys, 'ctx', axis=0, tiled=True)  28.6 us
    all_gather x1, blocking collectives, local(): now_k = lax.all_gather(key_now, 'ctx', axis=0, tiled=True)  25.1 us
    all_gather x1, blocking collectives, local(): now_v = lax.all_gather(value_now, 'ctx', axis=0, tiled=True)  24.4 us
  transfers between devices with their start and end apart: 8, of which 7 were waited for; matrix products, arithmetic and copies ran while one was open for 5% of the time, Pallas kernels for 0%

commit v1 on v0

--- a/solution.py
+++ b/solution.py
@@ -1,13 +1,200 @@
+import functools
 import math
 
 import jax
 import jax.numpy as jnp
 from jax import lax
+from jax.experimental import pallas as pl
+from jax.experimental.pallas import tpu as pltpu
 from jax.sharding import PartitionSpec as P
 
 HEADS = 32
 KV_HEADS = 8
 HEAD_DIM = 128
+MESH = pl.DeviceIdType.MESH
+NX, NY, NK = 4, 2, 2
+
+Y_THEN_X = (
+    (None, (0, 0, 0), None, "Y"),
+    (None, (0, 0, 0), None, "R"),
+    (None, (0, 0, 0), None, "L"),
+    (None, (0, 0, 0), None, "S"),
+    (0, (0, 1, 0), None, "R"),
+    (0, (0, 1, 0), None, "L"),
+    (0, (0, 1, 0), None, "S"),
+    (1, (-1, 0, 0), 0, "R"),
+    (1, (-1, 0, 0), None, "S"),
+    (2, (1, 0, 0), 1, "L"),
+    (2, (1, 0, 0), None, "S"),
+    (4, (-1, 1, 0), 0, "R"),
+    (4, (-1, 1, 0), None, "S"),
+    (5, (1, 1, 0), 1, "L"),
+    (5, (1, 1, 0), None, "S"),
+    (7, (2, 0, 0), 0, "S"),
+    (9, (2, 0, 0), 1, "S"),
+    (11, (2, 1, 0), 0, "S"),
+    (13, (2, 1, 0), 1, "S"),
+)
+X_THEN_Y = (
+    (None, (0, 0, 0), None, "R"),
+    (None, (0, 0, 0), None, "L"),
+    (None, (0, 0, 0), None, "Y"),
+    (None, (0, 0, 0), None, "S"),
+    (0, (-1, 0, 0), 0, "R"),
+    (0, (-1, 0, 0), None, "Y"),
+    (0, (-1, 0, 0), None, "S"),
+    (1, (1, 0, 0), 1, "L"),
+    (1, (1, 0, 0), None, "Y"),
+    (1, (1, 0, 0), None, "S"),
+    (2, (0, 1, 0), None, "S"),
+    (4, (2, 0, 0), 0, "Y"),
+    (4, (2, 0, 0), 0, "S"),
+    (7, (2, 0, 0), 1, "Y"),
+    (7, (2, 0, 0), 1, "S"),
+    (5, (-1, 1, 0), None, "S"),
+    (8, (1, 1, 0), None, "S"),
+    (11, (2, 1, 0), 0, "S"),
+    (13, (2, 1, 0), 1, "S"),
+)
+N_TRANSFERS = 19
+STEP = {"R": (1, 0, 0), "L": (-1, 0, 0), "Y": (0, 1, 0), "S": (0, 0, 1)}
+FROM = {"R": (-1, 0, 0), "L": (1, 0, 0), "Y": (0, 1, 0), "S": (0, 0, 1)}
+
+
+def ctx_at(delta):
+    c = lax.axis_index("ctx")
+    x = (c // 4 + delta[0] + NX) % NX
+    y = ((c // 2) % 2 + delta[1]) % NY
+    k = (c % 2 + delta[2]) % NK
+    return x * 4 + y * 2 + k
+
+
+def plus(a, b):
+    return ((a[0] + b[0]) % NX, (a[1] + b[1]) % NY, (a[2] + b[2]) % NK)
+
+
+def greet(targets):
+    barrier = pltpu.get_barrier_semaphore()
+    for target in targets:
+        pl.semaphore_signal(barrier, inc=1, device_id=target, device_id_type=MESH)
+    pl.semaphore_wait(barrier, len(targets))
+
+
+def ctx_neighbours():
+    e = lax.axis_index("exp")
+    return [(ctx_at(STEP[t]), e) for t in "RLYS"]
+
+
+class Gather:
+    def __init__(self, number, mode, own, slot, send, recv):
+        self.number, self.mode, self.own, self.slot = number, mode, own, slot
+        self.send, self.recv = send, recv
+        self.depth = []
+        for trigger, _, _, _ in mode:
+            self.depth.append(0 if trigger is None else self.depth[trigger] + 1)
+
+    def copy(self, j, arriving):
+        trigger, rel, half, to = self.mode[j]
+        e = lax.axis_index("exp")
+        at = plus(FROM[to], rel) if arriving else rel
+        ref = self.slot(ctx_at(at), half)
+        source = self.own if trigger is None and not arriving else ref
+        return pltpu.make_async_remote_copy(
+            src_ref=source,
+            dst_ref=ref,
+            send_sem=self.send.at[self.number, j],
+            recv_sem=self.recv.at[self.number, j],
+            device_id=(ctx_at(STEP[to]), e),
+            device_id_type=MESH,
+        )
+
+    def start(self, trigger):
+        for j, transfer in enumerate(self.mode):
+            if transfer[0] == trigger:
+                self.copy(j, False).start()
+
+    def arrive(self, j):
+        self.copy(j, True).wait_recv()
+
+    def events(self):
+        triggers = sorted({t[0] for t in self.mode if t[0] is not None})
+        out = [(0, functools.partial(self.start, None))]
+
+        def forward(j):
+            self.arrive(j)
+            self.start(j)
+
+        for j in triggers:
+            out.append((self.depth[j] + 1, functools.partial(forward, j)))
+        return out
+
+    def finish(self):
+        forwarded = {t[0] for t in self.mode}
+        for j in range(len(self.mode)):
+            if j not in forwarded:
+                self.arrive(j)
+
+    def drain(self):
+        for j in range(len(self.mode)):
+            self.copy(j, False).wait_send()
+
+
+def run_gathers(pieces, lag=1.0):
+    events = []
+    for piece in pieces:
+        for order, (depth, action) in enumerate(piece.events()):
+            events.append((piece.number + lag * depth, order, piece.number, action))
+    for _, _, _, action in sorted(events, key=lambda ev: ev[:3]):
+        action()
+    for piece in pieces:
+        piece.finish()
+    for piece in pieces:
+        piece.drain()
+
+
+def halves_of(ref, index_rows, rows, half, axis):
+    return ref
+
+
+def gather_kernel(plan, count, *refs):
+    ins, outs = refs[:count], refs[count:2 * count]
+    send, recv, local = refs[2 * count:]
+    greet(ctx_neighbours())
+    pieces, copies = [], []
+    for number, (a, mode, first, rows) in enumerate(plan):
+        out, width = outs[a], ins[a].shape[1]
+
+        def slot(index, half, out=out, first=first, rows=rows, width=width):
+            if half is None:
+                return out.at[index, pl.ds(first, rows), :]
+            part = rows // 2
+            return out.at[index, pl.ds(first + half * part, part), :]
+
+        own = ins[a].at[pl.ds(first, rows), :]
+        pieces.append(Gather(number, mode, own, slot, send, recv))
+        copies.append(pltpu.make_async_copy(own, slot(lax.axis_index("ctx"), None), local.at[number]))
+    for copy in copies:
+        copy.start()
+    run_gathers(pieces)
+    for copy in copies:
+        copy.wait()
+
+
+def gather_ctx(arrays, plan, collective_id, name):
+    n = len(plan)
+    return pl.pallas_call(
+        functools.partial(gather_kernel, plan, len(arrays)),
+        out_shape=[jax.ShapeDtypeStruct((16,) + a.shape, a.dtype) for a in arrays],
+        in_specs=[pl.BlockSpec(memory_space=pl.ANY)] * len(arrays),
+        out_specs=[pl.BlockSpec(memory_space=pl.ANY)] * len(arrays),
+        scratch_shapes=[
+            pltpu.SemaphoreType.DMA((n, N_TRANSFERS)),
+            pltpu.SemaphoreType.DMA((n, N_TRANSFERS)),
+            pltpu.SemaphoreType.DMA((n,)),
+        ],
+        compiler_params=pltpu.CompilerParams(collective_id=collective_id, has_side_effects=True),
+        name=name,
+    )(*arrays)
 
 
 def rms_scale(matrix, gain_vec):
@@ -66,11 +253,19 @@
     kv_local = key_width // HEAD_DIM
     head_group = HEADS // KV_HEADS
     normed = rms_scale(hidden_in, attn_gain)
-    portions = (
-        lax.all_gather(w_query, "ctx", axis=0, tiled=True),
-        lax.all_gather(w_key, "ctx", axis=0, tiled=True),
-        lax.all_gather(w_value, "ctx", axis=0, tiled=True),
-    )
+    a, b = Y_THEN_X, X_THEN_Y
+    gathered = gather_ctx(
+        (w_key, w_value, w_query, prior_keys, prior_values, w_out),
+        (
+            (0, a, 0, 256), (1, b, 0, 256), (2, a, 0, 128), (2, b, 128, 128), (3, a, 0, 128), (4, b, 0, 128),
+            (5, a, 0, 256), (5, b, 256, 256),
+        ),
+        0,
+        "gather_weights",
+    )
+    portions = tuple(gathered[i].reshape(-1, gathered[i].shape[-1]) for i in (2, 0, 1))
+    prior_k, prior_v = (gathered[i].reshape(-1, HEAD_DIM) for i in (3, 4))
+    w_out_all = gathered[5].transpose(1, 0, 2).reshape(w_out.shape[0], -1)
     query_raw, key_raw, value_raw = tuple(
         (jnp.dot(normed, portion, preferred_element_type=jnp.float32) for portion in portions)
     )
@@ -87,10 +282,8 @@
         ctx_index * local_len + jnp.arange(local_len * head_group, dtype=jnp.int32) // head_group
     )
     row_best = jnp.full((kv_local, local_len * head_group), -1e30, jnp.float32)
-    prior_k = lax.all_gather(prior_keys, "ctx", axis=0, tiled=True)
-    prior_v = lax.all_gather(prior_values, "ctx", axis=0, tiled=True)
-    now_k = lax.all_gather(key_now, "ctx", axis=0, tiled=True)
-    now_v = lax.all_gather(value_now, "ctx", axis=0, tiled=True)
+    now_k, now_v = gather_ctx((key_now, value_now), ((0, a, 0, 128), (1, b, 0, 128)), 1, "gather_kv")
+    now_k, now_v = now_k.reshape(-1, key_width), now_v.reshape(-1, key_width)
     key_span = prior_k.shape[0]
     key_index = jnp.arange(key_span, dtype=jnp.int32)
     keys_cat = jnp.concatenate([prior_k, now_k], axis=0).reshape(2 * key_span, kv_local, HEAD_DIM)
@@ -118,7 +311,7 @@
     )
     head_part = jnp.dot(
         attended,
-        lax.all_gather(w_out, "ctx", axis=1, tiled=True),
+        w_out_all,
         preferred_element_type=jnp.float32,
     )
     summed = lax.psum_scatter(
@@ -149,7 +342,12 @@
     gate_mat = w_gate[0]
     up_mat = w_up[0]
     down_mat = w_down[0]
-    flattened = lax.all_gather(arrived, "ctx", axis=0, tiled=True).reshape(-1, model_width)
+    flattened = gather_ctx(
+        (arrived.reshape(-1, model_width),),
+        ((0, a, 0, 32), (0, b, 32, 32)),
+        2,
+        "gather_tokens",
+    )[0].reshape(-1, model_width)
     gate_part = jnp.dot(flattened, gate_mat, preferred_element_type=jnp.float32)
     up_part = jnp.dot(flattened, up_mat, preferred_element_type=jnp.float32)
     hidden_act = (jax.nn.silu(gate_part) * up_part).astype(jnp.bfloat16)

time: 508 us -> 361 us (0.71)
  waiting for transfers between devices: 310 us -> 136 us
  Pallas kernels: 0 us -> 114 us
  blocking collectives: 111 us -> 10.6 us
  local copies, waits for them, and re-layouts: 2.74 us -> 14 us
    all_gather x5 -> x0, waiting for transfers between devices: 169 us -> none  [the longest x1 78 us: local(): lax.all_gather(arrived, 'ctx', axis=0, tiled=True).reshape(-1, model_width)]
    pallas_call x0 -> x3, Pallas kernels: none -> 114 us  [gather_ctx(): pl.pallas_call(functools.partial(gather_kernel, plan, len(arrays)), out_s...]
    all_gather x4 -> x0, blocking collectives: 100 us -> none  [the longest x1 28.6 us: local(): prior_k = lax.all_gather(prior_keys, 'ctx', axis=0, tiled=True)]
    transpose x0 -> x1, local copies, waits for them, and re-layouts: none -> 6.45 us  [local(): w_out_all = gathered[5].transpose(1, 0, 2).reshape(w_out.shape[0], -1)]
    dot_general x0 -> x1, local copies, waits for them, and re-layouts: none -> 6.39 us  [local(): jnp.dot(normed, portion, preferred_element_type=jnp.float32)]
  transfers between devices with their start and end apart: 8 -> 3, of which waited for: 7 -> 3; matrix products, arithmetic and copies ran while one was open for 5% -> 0% of each run, Pallas kernels for 0% -> 0%
where the time goes in v1:
time: 361 us; the launch traced here: 358 us
  waiting for transfers between devices  136 us (38%)
  Pallas kernels  114 us (32%)
  matrix products  54.4 us (15%)
  between operations  14.4 us (4%)
  local copies, waits for them, and re-layouts  14 us (4%)
  blocking collectives  10.6 us (3%)
  other arithmetic  9.96 us (3%)
  starting transfers between devices  4.25 us (1%)
    pallas_call x3, Pallas kernels, gather_ctx(): pl.pallas_call(functools.partial(gather_kernel, plan, len(arrays)), out_s...  114 us
    reduce_scatter x1, waiting for transfers between devices, local(): lax.psum_scatter(jnp.dot(hidden_act, down_mat, preferred_element_type=jnp...  96.1 us
    reduce_scatter x1, waiting for transfers between devices, local(): lax.psum_scatter(head_part.astype(jnp.bfloat16), 'exp', scatter_dimension...  32.8 us
    dot_general x1, matrix products, local(): up_part = jnp.dot(flattened, up_mat, preferred_element_type=jnp.float32)  12.5 us
    dot_general x1, matrix products, local(): gate_part = jnp.dot(flattened, gate_mat, preferred_element_type=jnp.float32)  12.1 us
    dot_general x1, matrix products, local(): jnp.dot(hidden_act, down_mat, preferred_element_type=jnp.float32)  11.1 us
    all_to_all x1, blocking collectives, local(): lax.all_to_all(outgoing, 'exp', split_axis=0, concat_axis=0, tiled=True)  10.6 us
    dot_general x3, matrix products, local(): jnp.dot(normed, portion, preferred_element_type=jnp.float32)  7.89 us
  transfers between devices with their start and end apart: 3, of which 3 were waited for; matrix products, arithmetic and copies ran while one was open for 0% of the time, Pallas kernels for 0%

profile of v1, /device:TPU:1, one launch (start us, length us, event | category | flops | bytes accessed | tf_op | source)
XLA Modules:
  0.0 357.9 jit_solution(5569230042183272028)
XLA Ops:
  6.5 0.8 convert_element_type.89
  7.3 1.5 fusion.13
  9.6 0.2 multiply_cosine_fusion.1
  9.8 54.5 %gather_weights.1 = (bf16[16,256,128]{2,1,0:T(8,128)(2,1)}, bf16[16,256,128]{2,1,0:T(8,128)(2,1)}, bf16[16,256,512]{2,1,0:T(8,128)(2,1)}, bf16[16,128,128]{2,1,0...) custom-call(bf16[256,128]{1,0:T(8,128)(2,1)} %refs_0_.1, bf16[256,128]{1,0:T(8,128)(2,1)} %refs_1_.1, ...), custom_call_target="tpu_custom_call" | custom-call | tf_op jit(solution)/shard_map/gather_weights/pallas_call | solution.py:185
  64.3 2.0 convolution_bitcast_fusion
  66.3 0.3 fusion.45
  66.6 2.3 convolution_convert_fusion.3.refs_1_
  69.0 6.4 %copy.27 = bf16[512,4096]{1,0:T(8,128)(2,1)} copy(bf16[512,4096]{0,1:T(8,128)(2,1)} %bitcast.57) | data formatting | bytes 8388608 | tf_op jit(solution)/shard_map/dot_general | solution.py:270
  75.4 3.5 fusion.30
  79.2 1.4 iota_compare_fusion.1
  80.6 0.7 maximum_bitcast_fusion.refs_0_
  81.3 15.9 %gather_kv.1 = (bf16[16,128,128]{2,1,0:T(8,128)(2,1)}, bf16[16,128,128]{2,1,0:T(8,128)(2,1)}) custom-call(bf16[128,128]{1,0:T(8,128)(2,1)} %maximum_bitcast_fusion.refs_0_, bf16[128,128]{1,0:T(8,128)(2,1)} %convolution_convert_fusion.3.refs_1_), custom_call_target="tpu_custom_call" | custom-call | tf_op jit(solution)/shard_map/gather_kv/pallas_call | solution.py:185
  97.2 3.3 fusion
  100.5 2.8 fusion.6
  103.3 2.3 fusion.20
  105.7 6.4 %copy.32 = bf16[512,16,256]{0,2,1:T(8,128)(2,1)} copy(bf16[512,16,256]{2,0,1:T(8,128)(2,1)} %bitcast.56) | data formatting | bytes 8388608 | tf_op jit(solution)/shard_map/transpose | solution.py:268
  112.2 4.7 %convolution_convert_fusion.1 = bf16[128,4096]{1,0:T(8,128)(2,1)} fusion(bf16[128,512]{1,0:T(8,128)(2,1)S(1)} %convert_element_type.97, bf16[512,4096]{0,1:T(8,128)(2,1)} %bitcast.53), kind=kOutput, calls=%fused_computation.12 | convolution fusion | flops 537395200 | bytes 5373952 | tf_op jit(solution)/shard_map/dot_general | solution.py:312
  117.3 0.2 select_reduce_fusion
  117.5 32.8 %reduce-scatter.3.cloned.1.call-done = bf16[16,4096]{1,0:T(8,128)(2,1)} async-done(((bf16[128,4096]{1,0:T(8,128)(2,1)}), bf16[16,4096]{1,0:T(8,128)(2,1)}) %reduce-scatter.3.cloned.1.call-update) | async-done | bytes 131088 | tf_op jit(solution)/shard_map/reduce_scatter | solution.py:317
  150.3 1.1 fusion.33
  151.5 0.2 broadcast_in_dim.13
  151.8 0.3 fusion.8
  152.1 10.6 %all_to_all.10 = bf16[8,8,4096]{2,1,0:T(8,128)(2,1)} all-to-all(bf16[8,8,4096]{2,1,0:T(8,128)(2,1)S(1)} %fusion.8), channel_id=1, replica_groups=mesh['ctx'=16,'exp'=8] {'exp'}, dimensions={0} | all-to-all | bytes 1048576 | tf_op jit(solution)/shard_map/all_to_all | solution.py:341
  162.7 44.1 %gather_tokens.1 = bf16[16,64,4096]{2,1,0:T(8,128)(2,1)} custom-call(bf16[64,4096]{1,0:T(8,128)(2,1)} %bitcast.59), custom_call_target="tpu_custom_call" | custom-call | tf_op jit(solution)/shard_map/gather_tokens/pallas_call | solution.py:185
  206.8 12.5 %fusion.2 = f32[1024,896]{1,0:T(8,128)S(1)} fusion(bf16[1024,4096]{1,0:T(8,128)(2,1)} %bitcast.54, bf16[1,4096,896]{2,1,0:T(8,128)(2,1)} %param.26), kind=kOutput, calls=%fused_computation.6 | convolution fusion | flops 7516192768 | bytes 19398656 | tf_op jit(solution)/shard_map/dot_general | solution.py:352
  219.4 12.1 %multiply_convert_fusion = bf16[1024,896]{1,0:T(8,128)(2,1)S(1)} fusion(f32[1024,896]{1,0:T(8,128)S(1)} %fusion.2, bf16[1024,4096]{1,0:T(8,128)(2,1)S(1)} %bitcast.55, bf16[1,4096,896]{2,1,0:T(8,128)(2,1)} %param.25), kind=kOutput, calls=%fused_computation.19 | convolution fusion | flops 7521697792 | bytes 21233664 | tf_op jit(solution)/shard_map/dot_general | solution.py:351
  231.5 11.1 %convolution_convert_fusion = bf16[1024,4096]{1,0:T(8,128)(2,1)} fusion(bf16[1024,896]{1,0:T(8,128)(2,1)S(1)} %multiply_convert_fusion, bf16[1,896,4096]{2,1,0:T(8,128)(2,1)S(1)} %bitcast.64), kind=kOutput, calls=%fused_computation.3 | convolution fusion | flops 7520387072 | bytes 17563648 | tf_op jit(solution)/shard_map/dot_general | solution.py:355
  242.6 96.1 %reduce-scatter.5.cloned.1.call-done = bf16[64,4096]{1,0:T(8,128)(2,1)} async-done(((bf16[1024,4096]{1,0:T(8,128)(2,1)}), bf16[64,4096]{1,0:T(8,128)(2,1)}) %reduce-scatter.5.cloned.1.call-update) | async-done | bytes 524304 | tf_op jit(solution)/shard_map/reduce_scatter | solution.py:354
  338.7 4.2 %all-to-all-start.1 = ((bf16[8,8,4096]{2,1,0:T(8,128)(2,1)}), bf16[8,8,4096]{2,1,0:T(8,128)(2,1)S(1)}, u32[]{:S(2)}, u32[]{:S(2)}) async-start(bf16[8,8,4096]{2,1,0:T(8,128)(2,1)} %bitcast.60), calls=%async_computation.3 | async-start | bytes 1048576 | tf_op jit(solution)/shard_map/all_to_all | solution.py:361
  343.1 7.0 %all-to-all-done.1 = bf16[8,8,4096]{2,1,0:T(8,128)(2,1)S(1)} async-done(((bf16[8,8,4096]{2,1,0:T(8,128)(2,1)}), bf16[8,8,4096]{2,1,0:T(8,128)(2,1)S(1)}, u32[]{:S(2)}, u32[]{:S(2)}) %all-to-all-start.1) | async-done | bytes 524320 | tf_op jit(solution)/shard_map/all_to_all | solution.py:361
  350.1 0.3 fusion.16
  350.4 0.7 fusion.36
  (46 shorter events, 1.3 us)
Async XLA Ops:
  6.5 110.4 %copy-start = (s32[2048,2]{0,1:T(2,128)S(1)}, s32[2048,2]{0,1:T(2,128)}, u32[]{:S(2)}) copy-start(s32[2048,2]{0,1:T(2,128)} %param.28) | copy-start | bytes 49156
  6.5 60.1 %copy-start.3 = (bf16[128,4096]{1,0:T(8,128)(2,1)S(1)}, bf16[128,4096]{1,0:T(8,128)(2,1)}, u32[]{:S(2)}) copy-start(bf16[128,4096]{1,0:T(8,128)(2,1)} %param.15) | copy-start | bytes 3145732
  6.5 143.7 %reduce-scatter.3.cloned.1.call-start = ((), (), s32[]{:S(2)}) async-start(), calls=%async_computation.4 | async-start | bytes 1179648 | tf_op jit(solution)/shard_map/reduce_scatter | solution.py:317
  100.5 2.8 copy-start.6
  100.5 2.8 copy-start.7
  112.2 4.7 %copy-start.4 = (bf16[4096]{0:T(1024)(128)(2,1)S(1)}, bf16[4096]{0:T(1024)(128)(2,1)}, u32[]{:S(2)}) copy-start(bf16[4096]{0:T(1024)(128)(2,1)} %param.24) | copy-start | bytes 24580
  116.9 221.8 %reduce-scatter.5.cloned.1.call-start = ((), (), s32[]{:S(2)}) async-start(), calls=%async_computation.5 | async-start | bytes 8912896 | tf_op jit(solution)/shard_map/reduce_scatter | solution.py:354
  206.8 12.5 %copy-start.2 = (bf16[16,64,4096]{2,1,0:T(8,128)(2,1)S(1)}, bf16[16,64,4096]{2,1,0:T(8,128)(2,1)}, u32[]{:S(2)}) copy-start(bf16[16,64,4096]{2,1,0:T(8,128)(2,1)} %gather_tokens.1) | copy-start | bytes 25165828
  206.8 24.6 %slice-start = ((s8[7340032]{0:T(1024)(128)(4,1)}), s8[4194304]{0:T(1024)(128)(4,1)S(1)}, s32[]{:S(2)}) async-start(s8[7340032]{0:T(1024)(128)(4,1)} %bitcast.63), calls=%async_computation.6 | async-start | bytes 8388608
  219.4 12.1 %slice-start.1 = ((s8[7340032]{0:T(1024)(128)(4,1)}), s8[3145728]{0:T(1024)(128)(4,1)S(1)}, s32[]{:S(2)}) async-start(s8[7340032]{0:T(1024)(128)(4,1)} %bitcast.63), calls=%async_computation.7 | async-start | bytes 6291456
  242.5 108.5 %copy-start.1 = (s32[2048,2]{0,1:T(2,128)S(1)}, s32[2048,2]{0,1:T(2,128)}, u32[]{:S(2)}) copy-start(s32[2048,2]{0,1:T(2,128)} %param.28) | copy-start | bytes 49156
  242.5 107.5 %copy-start.5 = (f32[16,2]{0,1:T(2,128)S(1)}, f32[16,2]{0,1:T(2,128)}, u32[]{:S(2)}) copy-start(f32[16,2]{0,1:T(2,128)} %param.29) | copy-start | bytes 388
  338.7 11.4 %all-to-all-start.1 = ((bf16[8,8,4096]{2,1,0:T(8,128)(2,1)}), bf16[8,8,4096]{2,1,0:T(8,128)(2,1)S(1)}, u32[]{:S(2)}, u32[]{:S(2)}) async-start(bf16[8,8,4096]{2,1,0:T(8,128)(2,1)} %bitcast.60), calls=%async_computation.3 | async-start | bytes 1048576 | tf_op jit(solution)/shard_map/all_to_all | solution.py:361
Sparse Core Ops, SparseCore 0:
  117.0 33.2 reduce-scatter.2
  242.7 95.9 reduce-scatter.4

commit v2 on v1

v2 whole, which is shorter than its diff:
```python
import functools
import math

import jax
import jax.numpy as jnp
from jax import lax
from jax.experimental import pallas as pl
from jax.experimental.pallas import tpu as pltpu
from jax.sharding import PartitionSpec as P

HEADS = 32
KV_HEADS = 8
HEAD_DIM = 128
MESH = pl.DeviceIdType.MESH
NX, NY, NK = 4, 2, 2

Y_THEN_X = (
    (None, (0, 0, 0), None, "Y"),
    (None, (0, 0, 0), None, "R"),
    (None, (0, 0, 0), None, "L"),
    (None, (0, 0, 0), None, "S"),
    (0, (0, 1, 0), None, "R"),
    (0, (0, 1, 0), None, "L"),
    (0, (0, 1, 0), None, "S"),
    (1, (-1, 0, 0), 0, "R"),
    (1, (-1, 0, 0), None, "S"),
    (2, (1, 0, 0), 1, "L"),
    (2, (1, 0, 0), None, "S"),
    (4, (-1, 1, 0), 0, "R"),
    (4, (-1, 1, 0), None, "S"),
    (5, (1, 1, 0), 1, "L"),
    (5, (1, 1, 0), None, "S"),
    (7, (2, 0, 0), 0, "S"),
    (9, (2, 0, 0), 1, "S"),
    (11, (2, 1, 0), 0, "S"),
    (13, (2, 1, 0), 1, "S"),
)
X_THEN_Y = (
    (None, (0, 0, 0), None, "R"),
    (None, (0, 0, 0), None, "L"),
    (None, (0, 0, 0), None, "Y"),
    (None, (0, 0, 0), None, "S"),
    (0, (-1, 0, 0), 0, "R"),
    (0, (-1, 0, 0), None, "Y"),
    (0, (-1, 0, 0), None, "S"),
    (1, (1, 0, 0), 1, "L"),
    (1, (1, 0, 0), None, "Y"),
    (1, (1, 0, 0), None, "S"),
    (2, (0, 1, 0), None, "S"),
    (4, (2, 0, 0), 0, "Y"),
    (4, (2, 0, 0), 0, "S"),
    (7, (2, 0, 0), 1, "Y"),
    (7, (2, 0, 0), 1, "S"),
    (5, (-1, 1, 0), None, "S"),
    (8, (1, 1, 0), None, "S"),
    (11, (2, 1, 0), 0, "S"),
    (13, (2, 1, 0), 1, "S"),
)
DIRECT = tuple((None, (0, 0, 0), None, to) for to in ("R", "L", "Y", "O", "RY", "LY", "OY", "S")) + (
    (0, (-1, 0, 0), None, "S"),
    (1, (1, 0, 0), None, "S"),
    (2, (0, 1, 0), None, "S"),
    (3, (2, 0, 0), None, "S"),
    (4, (-1, 1, 0), None, "S"),
    (5, (1, 1, 0), None, "S"),
    (6, (2, 1, 0), None, "S"),
)
N_TRANSFERS = 19
STEP = {
    "R": (1, 0, 0), "L": (-1, 0, 0), "Y": (0, 1, 0), "S": (0, 0, 1),
    "O": (2, 0, 0), "RY": (1, 1, 0), "LY": (-1, 1, 0), "OY": (2, 1, 0),
}
FROM = {to: (-step[0], step[1], step[2]) for to, step in STEP.items()}


def ctx_at(delta):
    c = lax.axis_index("ctx")
    x = (c // 4 + delta[0] + NX) % NX
    y = ((c // 2) % 2 + delta[1]) % NY
    k = (c % 2 + delta[2]) % NK
    return x * 4 + y * 2 + k


def plus(a, b):
    return ((a[0] + b[0]) % NX, (a[1] + b[1]) % NY, (a[2] + b[2]) % NK)


def greet(targets):
    barrier = pltpu.get_barrier_semaphore()
    for target in targets:
        pl.semaphore_signal(barrier, inc=1, device_id=target, device_id_type=MESH)
    pl.semaphore_wait(barrier, len(targets))


def ctx_neighbours():
    e = lax.axis_index("exp")
    return [(ctx_at(STEP[t]), e) for t in "RLYS"]


class Gather:
    def __init__(self, number, mode, slot, send, recv):
        self.number, self.mode, self.slot = number, mode, slot
        self.send, self.recv = send, recv
        self.depth = []
        for trigger, _, _, _ in mode:
            self.depth.append(0 if trigger is None else self.depth[trigger] + 1)

    def copy(self, j, arriving):
        trigger, rel, half, to = self.mode[j]
        e = lax.axis_index("exp")
        at = plus(FROM[to], rel) if arriving else rel
        ref = self.slot(ctx_at(at), half)
        source = ref
        return pltpu.make_async_remote_copy(
            src_ref=source,
            dst_ref=ref,
            send_sem=self.send.at[self.number, j],
            recv_sem=self.recv.at[self.number, j],
            device_id=(ctx_at(STEP[to]), e),
            device_id_type=MESH,
        )

    def start(self, trigger):
        for j, transfer in enumerate(self.mode):
            if transfer[0] == trigger:
                self.copy(j, False).start()

    def arrive(self, j):
        self.copy(j, True).wait_recv()

    def events(self):
        triggers = sorted({t[0] for t in self.mode if t[0] is not None})
        out = [(0, functools.partial(self.start, None))]

        def forward(j):
            self.arrive(j)
            self.start(j)

        for j in triggers:
            out.append((self.depth[j] + 1, functools.partial(forward, j)))
        return out

    def finish(self):
        forwarded = {t[0] for t in self.mode}
        for j in range(len(self.mode)):
            if j not in forwarded:
                self.arrive(j)

    def drain(self):
        for j in range(len(self.mode)):
            self.copy(j, False).wait_send()


CHUNKS = (((0, 0), (0, 1)), ((3, 0), (1, 0)), ((3, 1), (1, 1)), ((2, 0), (2, 1)))
PLACE = {}
for _g, _pair in enumerate(CHUNKS):
    for _i, _xy in enumerate(_pair):
        for _dk in range(2):
            PLACE[_xy + (_dk,)] = (_g, _dk * 2 + _i)
ROWS = 64
GU = 128
DN = 512


class LocalGather(Gather):
    def copy(self, j, arriving):
        trigger, rel, half, to = self.mode[j]
        e = lax.axis_index("exp")
        there = plus(FROM[to], rel)
        here = there if arriving else plus(rel, (0, 0, 0))
        return pltpu.make_async_remote_copy(
            src_ref=self.slot(here, half),
            dst_ref=self.slot(there, half),
            send_sem=self.send.at[self.number, j],
            recv_sem=self.recv.at[self.number, j],
            device_id=(ctx_at(STEP[to]), e),
            device_id_type=MESH,
        )


def expert_kernel(
    arrived, gate, up, down, out,
    tok, wgu, wdn, hid, part, from_sib, from_x, from_y,
    ag_send, ag_recv, w_sem, own_sem, rs_send, rs_recv,
):
    e = lax.axis_index("exp")
    units = gate.shape[2] // GU
    width = down.shape[2]
    own_copy = pltpu.make_async_copy(arrived, tok.at[0, pl.ds(0, ROWS), :], own_sem)
    own_copy.start()
    loads = []
    for j in range(units):
        for s, w in enumerate((gate, up)):
            loads.append(
                pltpu.make_async_copy(
                    w.at[0, :, pl.ds(j * GU, GU)], wgu.at[j, :, pl.ds(s * GU, GU)], w_sem.at[2 * j + s]
                )
            )
    loads.append(pltpu.make_async_copy(down.at[0], wdn, w_sem.at[2 * units]))
    greet(ctx_neighbours() + [(ctx_at((2, 0, 0)), e)])
    own_copy.wait()

    pieces = []
    for number, mode in enumerate((Y_THEN_X, X_THEN_Y)):
        rows = ROWS // 2

        def slot(rel, half, first=number * rows, rows=rows):
            g, place = PLACE[rel]
            if half is None:
                return tok.at[g, pl.ds(place * ROWS + first, rows), :]
            return tok.at[g, pl.ds(place * ROWS + first + half * (rows // 2), rows // 2), :]

        pieces.append(LocalGather(number, mode, slot, ag_send, ag_recv))
    first, second = pieces
    for piece in pieces:
        piece.start(None)
    for load in loads:
        load.start()

    def forward(piece, *js):
        for j in js:
            piece.arrive(j)
            piece.start(j)

    def need(piece, *js):
        for j in js:
            piece.arrive(j)

    def gate_up(g, lo, hi):
        def body(j, _):
            both = jnp.dot(tok[g], wgu[j], preferred_element_type=jnp.float32)
            v = both[:, :GU]
            hid[:, pl.ds(pl.multiple_of(j * GU, GU), GU)] = (v / (1.0 + jnp.exp(-v)) * both[:, GU:]).astype(jnp.bfloat16)
            return 0

        lax.fori_loop(lo, hi, body, 0)

    def down_part(g, lo, hi):
        def body(n, _):
            cols = pl.ds(pl.multiple_of(n * DN, DN), DN)
            part[g, :, cols] = jnp.dot(hid[...], wdn[:, cols], preferred_element_type=jnp.float32).astype(jnp.bfloat16)
            return 0

        lax.fori_loop(lo, hi, body, 0)

    def rs_copy(j, source, target, to):
        return pltpu.make_async_remote_copy(
            src_ref=source, dst_ref=target, send_sem=rs_send.at[j], recv_sem=rs_recv.at[j],
            device_id=(ctx_at(to), e), device_id_type=MESH,
        )

    half = 2 * ROWS
    to_sib = [
        rs_copy(g, part.at[g, pl.ds(half, half), :], from_sib.at[g], (0, 0, 1)) for g in range(4)
    ]
    near, far = pl.ds(0, ROWS), pl.ds(ROWS, ROWS)
    to_x = {
        1: [
            rs_copy(4, part.at[1, near, :], from_x.at[0, 0], (-1, 0, 0)),
            rs_copy(5, part.at[1, far, :], from_x.at[1, 0], (1, 0, 0)),
        ],
        2: [
            rs_copy(6, part.at[2, near, :], from_x.at[0, 1], (-1, 0, 0)),
            rs_copy(7, part.at[2, far, :], from_x.at[1, 1], (1, 0, 0)),
        ],
        3: [
            rs_copy(8, part.at[3, far, :], from_x.at[2, 1], (2, 0, 0)),
            rs_copy(9, part.at[3, near, :], from_x.at[2, 0], (2, 0, 0)),
        ],
    }
    to_y = rs_copy(10, part.at[0, far, :], from_y, (0, 1, 0))
    tile = 16

    def add_rows(rows, terms, store):
        def body(i, _):
            at = pl.multiple_of(i * tile, tile)
            total = terms[0](at)
            for term in terms[1:]:
                total = total + term(at)
            store(at, total.astype(jnp.bfloat16))
            return 0

        lax.fori_loop(0, rows // tile, body, 0)

    def merge(g):
        to_sib[g].wait_recv()

        def store(at, value):
            part[g, pl.ds(at, tile), :] = value

        add_rows(
            half,
            [
                lambda at: part[g, pl.ds(at, tile), :].astype(jnp.float32),
                lambda at: from_sib[g, pl.ds(at, tile), :].astype(jnp.float32),
            ],
            store,
        )
        for copy in to_x.get(g, ()):
            copy.start()

    forward(first, 0)
    forward(second, 2)
    need(first, 3, 6)
    need(second, 3, 10)
    for load in loads[:-1]:
        load.wait()
    gate_up(0, 0, 4)
    forward(first, 1, 2)
    forward(second, 0, 1)
    gate_up(0, 4, units)
    loads[-1].wait()
    forward(first, 4, 5)
    down_part(0, 0, width // DN)
    to_sib[0].start()
    forward(second, 4, 7)
    forward(second, 5, 8)
    need(first, 8, 10)
    need(second, 6, 9)
    gate_up(1, 0, 4)
    forward(first, 7, 9)
    gate_up(1, 4, units)
    forward(second, 11, 13)
    down_part(1, 0, width // DN)
    to_sib[1].start()
    merge(0)
    forward(first, 11, 13)
    need(first, 12, 14)
    need(second, 15, 16)
    gate_up(2, 0, units)
    merge(1)
    down_part(2, 0, width // DN)
    to_sib[2].start()
    need(first, 15, 16, 17, 18)
    need(second, 12, 14, 17, 18)
    gate_up(3, 0, units)
    merge(2)
    down_part(3, 0, width // DN)
    to_sib[3].start()
    merge(3)

    to_x[2][0].wait_recv()
    to_x[2][1].wait_recv()
    to_x[3][0].wait_recv()

    def store_far(at, value):
        part[0, pl.ds(ROWS + at, tile), :] = value

    add_rows(
        ROWS,
        [lambda at: part[0, pl.ds(ROWS + at, tile), :].astype(jnp.float32)]
        + [lambda at, s=s: from_x[s, 1, pl.ds(at, tile), :].astype(jnp.float32) for s in range(3)],
        store_far,
    )
    to_y.start()
    to_x[1][0].wait_recv()
    to_x[1][1].wait_recv()
    to_x[3][1].wait_recv()
    to_y.wait_recv()

    def store_out(at, value):
        out[pl.ds(at, tile), :] = value

    add_rows(
        ROWS,
        [lambda at: part[0, pl.ds(at, tile), :].astype(jnp.float32)]
        + [lambda at, s=s: from_x[s, 0, pl.ds(at, tile), :].astype(jnp.float32) for s in range(3)]
        + [lambda at: from_y[pl.ds(at, tile), :].astype(jnp.float32)],
        store_out,
    )
    for piece in pieces:
        piece.drain()
    for copy in to_sib + to_x[1] + to_x[2] + to_x[3] + [to_y]:
        copy.wait_send()


def experts(arrived, w_gate, w_up, w_down):
    rows, width = arrived.shape
    ff = w_gate.shape[2]
    bf16 = jnp.bfloat16
    return pl.pallas_call(
        expert_kernel,
        out_shape=jax.ShapeDtypeStruct((rows, width), bf16),
        in_specs=[pl.BlockSpec(memory_space=pl.ANY)] * 4,
        out_specs=pl.BlockSpec(memory_space=pltpu.VMEM),
        scratch_shapes=[
            pltpu.VMEM((4, 4 * rows, width), bf16),
            pltpu.VMEM((ff // GU, width, 2 * GU), bf16),
            pltpu.VMEM((ff, width), bf16),
            pltpu.VMEM((4 * rows, ff), bf16),
            pltpu.VMEM((4, 4 * rows, width), bf16),
            pltpu.VMEM((4, 2 * rows, width), bf16),
            pltpu.VMEM((3, 2, rows, width), bf16),
            pltpu.VMEM((rows, width), bf16),
            pltpu.SemaphoreType.DMA((2, N_TRANSFERS)),
            pltpu.SemaphoreType.DMA((2, N_TRANSFERS)),
            pltpu.SemaphoreType.DMA((2 * (ff // GU) + 1,)),
            pltpu.SemaphoreType.DMA,
            pltpu.SemaphoreType.DMA((11,)),
            pltpu.SemaphoreType.DMA((11,)),
        ],
        compiler_params=pltpu.CompilerParams(
            collective_id=3, has_side_effects=True, vmem_limit_bytes=56 * 1024 * 1024
        ),
        name="experts",
    )(arrived, w_gate, w_up, w_down)

def mixer_kernel(
    hidden, attn_gain, w_query, w_key, w_value, w_out, prior_keys, prior_values, cosine, sine, ffn_gain,
    residual_out, normed_out,
    normed, wkv, wq, kv, wo, query, scores, best, mass, blend, attended, part, from_exp,
    send, recv, local, rs_send, rs_recv,
):
    c, e = lax.axis_index("ctx"), lax.axis_index("exp")
    f32, bf16 = jnp.float32, jnp.bfloat16
    tokens, width = hidden.shape
    depth = w_query.shape[0]
    heads = w_query.shape[1] // HEAD_DIM
    tok_dev = residual_out.shape[0]
    out_cols = w_out.shape[1]
    span = kv.shape[0] // 2

    own_rows = pl.ds(pl.multiple_of(c * depth, depth), depth)
    own_keys = pl.ds(pl.multiple_of(c * tokens, tokens), tokens)
    left, right = pl.ds(0, HEAD_DIM), pl.ds(HEAD_DIM, HEAD_DIM)
    copies = [
        pltpu.make_async_copy(source, target, local.at[i])
        for i, (source, target) in enumerate(
            (
                (w_key, wkv.at[own_rows, left]),
                (w_value, wkv.at[own_rows, right]),
                (prior_keys, kv.at[own_keys, left]),
                (prior_values, kv.at[own_keys, right]),
                (w_query, wq.at[own_rows, :]),
                (w_out, wo.at[c]),
            )
        )
    ]
    for copy in copies:
        copy.start()
    greet(
        [(ctx_at(step), e) for step in STEP.values()] + [(c, lax.rem(e + d, 8)) for d in range(1, 8)]
    )
    for copy in copies:
        copy.wait()

    def rows_of(buffer, stride, base, first, rows):
        def slot(index, half):
            part_rows = rows if half is None else rows // 2
            start = base + index * stride + first + (0 if half is None else half * part_rows)
            return buffer.at[pl.ds(pl.multiple_of(start, 16), part_rows), :]

        return slot

    def block_of(buffer, first, rows):
        def slot(index, half):
            part_rows = rows if half is None else rows // 2
            return buffer.at[index, pl.ds(first + (0 if half is None else half * part_rows), part_rows), :]

        return slot

    plan = []
    for buffer, stride in ((wkv, depth), (kv, tokens), (wq, depth)):
        for i, mode in enumerate((Y_THEN_X, X_THEN_Y)):
            plan.append((mode, rows_of(buffer, stride, 0, i * stride // 2, stride // 2)))
    for i, mode in enumerate((Y_THEN_X, X_THEN_Y)):
        rows = w_out.shape[0] // 2
        plan.append((mode, block_of(wo, i * rows, rows)))
    pieces = [Gather(n, mode, slot, send, recv) for n, (mode, slot) in enumerate(plan)]
    now = Gather(len(pieces), DIRECT, rows_of(kv, tokens, span, 0, tokens), send, recv)

    tile = 16

    def norm_rows(i, _):
        rows = pl.ds(pl.multiple_of(i * tile, tile), tile)
        wide = hidden[rows, :].astype(f32)
        inverse = lax.rsqrt(jnp.mean(wide * wide, axis=-1, keepdims=True) + 1e-05)
        normed[rows, :] = (wide * inverse * attn_gain[...].astype(f32)).astype(bf16)
        return 0

    def normalise():
        lax.fori_loop(0, tokens // tile, norm_rows, 0)

    def turned(a):
        return (a * cosine[...] + pltpu.roll(a, HEAD_DIM // 2, 1) * sine[...]).astype(bf16)

    def keys_and_values():
        for piece in pieces[:2]:
            piece.finish()
        both = jnp.dot(normed[...], wkv[...], preferred_element_type=f32)
        rows = pl.ds(pl.multiple_of(span + c * tokens, tokens), tokens)
        kv[rows, left] = turned(both[:, :HEAD_DIM])
        kv[rows, right] = both[:, HEAD_DIM:].astype(bf16)
        now.start(None)

    def queries():
        for piece in pieces[4:6]:
            piece.finish()
        for g in range(heads):
            raw = jnp.dot(normed[...], wq[:, pl.ds(g * HEAD_DIM, HEAD_DIM)], preferred_element_type=f32)
            query[pl.ds(g * tokens, tokens), :] = turned(raw)

    count = heads * tokens
    block = 2 * tokens
    blocks = span // block
    inverse_root = 1.0 / math.sqrt(HEAD_DIM)

    def score(start, size):
        keys = kv[pl.ds(pl.multiple_of(start, tokens), size), left]
        return lax.dot_general(query[...], keys, (((1,), (1,)), ((), ())), preferred_element_type=f32) * inverse_root

    def masks():
        row = lax.broadcasted_iota(jnp.int32, (count, tokens), 0) % tokens
        col = lax.broadcasted_iota(jnp.int32, (count, tokens), 1)
        return row, col

    def all_scores():
        for piece in pieces[2:4] + [now]:
            piece.finish()
        row, col = masks()
        first = score(c * tokens, block)
        head_part = jnp.where(col > row, first[:, :tokens], -1e30)
        scores[:, pl.ds(0, tokens)] = head_part
        scores[:, pl.ds(tokens, tokens)] = first[:, tokens:]
        last = jnp.where(col <= row, score(c * tokens + span, tokens), -1e30)
        scores[:, pl.ds(span, tokens)] = last
        best[...] = jnp.maximum(jnp.maximum(head_part, first[:, tokens:]), last)

        def body(b, _):
            s = score(c * tokens + b * block, block)
            scores[:, pl.ds(pl.multiple_of(b * block, block), block)] = s
            best[...] = jnp.maximum(best[...], jnp.maximum(s[:, :tokens], s[:, tokens:]))
            return 0

        lax.fori_loop(1, blocks, body, 0)
        best[...] = jnp.broadcast_to(jnp.max(best[...], axis=1, keepdims=True), best.shape)

    def blended():
        top = best[:, pl.ds(0, 1)]
        p = jnp.exp(scores[:, pl.ds(span, tokens)] - top)
        mass[...] = p
        values = kv[pl.ds(pl.multiple_of(c * tokens + span, tokens), tokens), right]
        blend[...] = jnp.dot(p.astype(bf16), values, preferred_element_type=f32)

        def body(b, _):
            p = jnp.exp(scores[:, pl.ds(pl.multiple_of(b * block, block), block)] - top)
            mass[...] += p[:, :tokens] + p[:, tokens:]
            values = kv[pl.ds(pl.multiple_of(c * tokens + b * block, tokens), block), right]
            blend[...] += jnp.dot(p.astype(bf16), values, preferred_element_type=f32)
            return 0

        lax.fori_loop(0, blocks, body, 0)
        result = (blend[...] / jnp.sum(mass[...], axis=1, keepdims=True)).astype(bf16)
        for g in range(heads):
            attended[:, pl.ds(g * HEAD_DIM, HEAD_DIM)] = result[g * tokens:(g + 1) * tokens, :]

    def forward_now():
        for j in range(7):
            now.arrive(j)
            now.start(j)

    timeline = []
    for piece in pieces:
        for order, (level, action) in enumerate(piece.events()):
            timeline.append((piece.number + 1.0 * level, order, action))
    timeline += [
        (1.5, 0, normalise),
        (4.5, 0, keys_and_values),
        (7.5, 0, forward_now),
        (8.5, 0, queries),
        (8.6, 0, all_scores),
        (9.5, 0, blended),
    ]
    for _, _, action in sorted(timeline, key=lambda item: item[:2]):
        action()
    for piece in pieces[6:]:
        piece.finish()

    def project(i, _):
        cols = pl.ds(pl.multiple_of(i * out_cols, out_cols), out_cols)
        part[:, cols] = jnp.dot(attended[...], wo[i], preferred_element_type=f32).astype(bf16)
        return 0

    lax.fori_loop(0, width // out_cols, project, 0)

    shares = []
    for d in range(1, 8):
        to = lax.rem(e + d, 8)
        shares.append(
            pltpu.make_async_remote_copy(
                src_ref=part.at[pl.ds(pl.multiple_of(to * tok_dev, tok_dev), tok_dev), :],
                dst_ref=from_exp.at[d - 1],
                send_sem=rs_send.at[d - 1],
                recv_sem=rs_recv.at[d - 1],
                device_id=(c, to),
                device_id_type=MESH,
            )
        )
    for share in shares:
        share.start()
    for share in shares:
        share.wait_recv()
    mine = pl.ds(pl.multiple_of(e * tok_dev, tok_dev), tok_dev)
    total = part[mine, :].astype(f32)
    for d in range(7):
        total = total + from_exp[d].astype(f32)
    residual = (hidden[mine, :].astype(f32) + total).astype(bf16)
    residual_out[...] = residual
    wide = residual.astype(f32)
    inverse = lax.rsqrt(jnp.mean(wide * wide, axis=-1, keepdims=True) + 1e-05)
    normed_out[...] = (wide * inverse * ffn_gain[...].astype(f32)).astype(bf16)
    for piece in pieces + [now]:
        piece.drain()
    for share in shares:
        share.wait_send()


def mixer(hidden, attn_gain, w_query, w_key, w_value, w_out, prior_keys, prior_values, cosine, sine, ffn_gain):
    tokens, width = hidden.shape
    depth, q_cols = w_query.shape
    bf16, f32 = jnp.bfloat16, jnp.float32
    span = 16 * tokens
    count = q_cols // HEAD_DIM * tokens
    vmem = pl.BlockSpec(memory_space=pltpu.VMEM)
    anywhere = pl.BlockSpec(memory_space=pl.ANY)
    return pl.pallas_call(
        mixer_kernel,
        out_shape=[jax.ShapeDtypeStruct((tokens // 8, width), bf16)] * 2,
        in_specs=[vmem, vmem] + [anywhere] * 6 + [vmem] * 3,
        out_specs=[vmem] * 2,
        scratch_shapes=[
            pltpu.VMEM((tokens, width), bf16),
            pltpu.VMEM((16 * depth, 2 * HEAD_DIM), bf16),
            pltpu.VMEM((16 * depth, q_cols), bf16),
            pltpu.VMEM((2 * span, 2 * HEAD_DIM), bf16),
            pltpu.VMEM((16,) + w_out.shape, bf16),
            pltpu.VMEM((count, HEAD_DIM), bf16),
            pltpu.VMEM((count, span + tokens), f32),
            pltpu.VMEM((count, tokens), f32),
            pltpu.VMEM((count, tokens), f32),
            pltpu.VMEM((count, HEAD_DIM), f32),
            pltpu.VMEM((tokens, q_cols), bf16),
            pltpu.VMEM((tokens, width), bf16),
            pltpu.VMEM((7, tokens // 8, width), bf16),
            pltpu.SemaphoreType.DMA((9, N_TRANSFERS)),
            pltpu.SemaphoreType.DMA((9, N_TRANSFERS)),
            pltpu.SemaphoreType.DMA((6,)),
            pltpu.SemaphoreType.DMA((7,)),
            pltpu.SemaphoreType.DMA((7,)),
        ],
        compiler_params=pltpu.CompilerParams(
            collective_id=0, has_side_effects=True, vmem_limit_bytes=48 * 1024 * 1024
        ),
        name="mixer",
    )(hidden, attn_gain, w_query, w_key, w_value, w_out, prior_keys, prior_values, cosine, sine, ffn_gain)


def local(
    hidden_in,
    attn_gain,
    w_query,
    w_key,
    w_value,
    w_out,
    prior_keys,
    prior_values,
    stretch_offset,
    ffn_gain,
    w_gate,
    w_up,
    w_down,
    expert_ids,
    gate_weights,
):
    exp_count = lax.axis_size("exp")
    ctx_index = lax.axis_index("ctx")
    exp_index = lax.axis_index("exp")
    local_len, model_width = hidden_in.shape
    tok_dev = local_len // exp_count
    positions = stretch_offset[0] + ctx_index * local_len + jnp.arange(local_len, dtype=jnp.int32)
    half_dim = HEAD_DIM // 2
    frequency = jnp.exp(jnp.arange(half_dim).astype(jnp.float32) * (-2.0 * math.log(1000000.0) / HEAD_DIM))
    angles = positions.astype(jnp.float32)[:, None] * frequency[None, :]
    cosine, sine = jnp.cos(angles), jnp.sin(angles)
    residual, normed_ffn = mixer(
        hidden_in,
        attn_gain[None],
        w_query,
        w_key,
        w_value,
        w_out,
        prior_keys,
        prior_values,
        jnp.concatenate([cosine, cosine], axis=1),
        jnp.concatenate([-sine, sine], axis=1),
        ffn_gain[None],
    )
    capacity = 4 * tok_dev // exp_count
    device_row = (ctx_index * exp_count + exp_index) * tok_dev
    my_ids = lax.dynamic_slice_in_dim(expert_ids, device_row, tok_dev, 0).reshape(-1)
    onehot = (my_ids[:, None] == jnp.arange(exp_count, dtype=jnp.int32)[None, :]).astype(jnp.int32)
    before = jnp.cumsum(onehot, axis=0) - onehot
    slot_of = jnp.sum(before * onehot, axis=1)
    slot_ids = jnp.arange(exp_count * capacity, dtype=jnp.int32)
    select = (
        (slot_ids[:, None] // capacity == my_ids[None, :])
        & (slot_ids[:, None] % capacity == slot_of[None, :])
    ).astype(jnp.bfloat16)
    repeated = jnp.repeat(normed_ffn, 2, axis=0)
    outgoing = (
        jnp.dot(select, repeated, preferred_element_type=jnp.float32)
        .astype(jnp.bfloat16)
        .reshape(exp_count, capacity, model_width)
    )
    arrived = lax.all_to_all(outgoing, "exp", split_axis=0, concat_axis=0, tiled=True)
    own_slots = experts(arrived.reshape(-1, model_width), w_gate, w_up, w_down)
    outcome = own_slots.reshape(exp_count, capacity, model_width)
    returned = lax.all_to_all(outcome, "exp", split_axis=0, concat_axis=0, tiled=True)
    gathered_back = jnp.dot(
        select.T,
        returned.reshape(exp_count * capacity, model_width),
        preferred_element_type=jnp.float32,
    )
    picked = gathered_back.reshape(tok_dev, 2, model_width)
    mixture = jnp.sum(gate_weights[:, :, None] * picked, axis=1)
    return (residual.astype(jnp.float32) + mixture).astype(jnp.bfloat16)


def solution(mesh):
    in_specs = (
        P("ctx", None),
        P(),
        P("ctx", "exp"),
        P("ctx", "exp"),
        P("ctx", "exp"),
        P("exp", "ctx"),
        P("ctx", "exp"),
        P("ctx", "exp"),
        P(),
        P(),
        P("exp", None, "ctx"),
        P("exp", None, "ctx"),
        P("exp", "ctx", None),
        P(),
        P(("ctx", "exp"), None),
    )
    out_specs = P(("ctx", "exp"), None)
    return jax.shard_map(local, mesh=mesh, in_specs=in_specs, out_specs=out_specs, check_vma=False)
```

time: 361 us -> 228 us (0.63)
  waiting for transfers between devices: 136 us -> 6.97 us
  Pallas kernels: 114 us -> 188 us
  matrix products: 54.4 us -> 0.62 us
  between operations: 14.4 us -> 0.78 us
  other arithmetic: 9.96 us -> 1.43 us
  local copies, waits for them, and re-layouts: 14 us -> 9.13 us
  blocking collectives: 10.6 us -> 14.9 us
    reduce_scatter x2 -> x0, waiting for transfers between devices: 129 us -> none  [the longest x1 96.1 us: local(): lax.psum_scatter(jnp.dot(hidden_act, down_mat, preferred_element_type=jnp...]
    pallas_call x3 -> x2, Pallas kernels: 114 us -> 188 us  [the longest x1 104 us: experts(): pl.pallas_call(expert_kernel, out_shape=jax.ShapeDtypeStruct((rows, width...]
    dot_general x9 -> x0, matrix products: 53.8 us -> none  [the longest x1 12.5 us: local(): up_part = jnp.dot(flattened, up_mat, preferred_element_type=jnp.float32)]
    unnamed x20 -> x18, local copies, waits for them, and re-layouts: 0.05 us -> 7.01 us
    transpose x1 -> x0, local copies, waits for them, and re-layouts: 6.45 us -> none  [local(): w_out_all = gathered[5].transpose(1, 0, 2).reshape(w_out.shape[0], -1)]
    dot_general x1 -> x0, local copies, waits for them, and re-layouts: 6.39 us -> none  [local(): jnp.dot(normed, portion, preferred_element_type=jnp.float32)]
    reduce_sum x3 -> x0, other arithmetic: 5.4 us -> none  [the longest x1 2.82 us: local(): row_mass = jnp.sum(weights, axis=2)]
    all_to_all x1, blocking collectives: 10.6 us -> 14.9 us  [local(): lax.all_to_all(outgoing, 'exp', split_axis=0, concat_axis=0, tiled=True)]
  transfers between devices with their start and end apart: 3 -> 1, of which waited for: 3 -> 1; matrix products, arithmetic and copies ran while one was open for 0% -> 0% of each run, Pallas kernels for 0% -> 0%
where the time goes in v2:
time: 228 us; the launch traced here: 227 us
  Pallas kernels  188 us (82%)
  blocking collectives  14.9 us (7%)
  local copies, waits for them, and re-layouts  9.13 us (4%)
  waiting for transfers between devices  6.97 us (3%)
  starting transfers between devices  5.86 us (3%)
    pallas_call x1, Pallas kernels, experts(): pl.pallas_call(expert_kernel, out_shape=jax.ShapeDtypeStruct((rows, width...  104 us
    pallas_call x1, Pallas kernels, mixer(): pl.pallas_call(mixer_kernel, out_shape=[jax.ShapeDtypeStruct((tokens // 8...  83.8 us
    all_to_all x1, blocking collectives, local(): lax.all_to_all(outgoing, 'exp', split_axis=0, concat_axis=0, tiled=True)  14.9 us
    unnamed x18, local copies, waits for them, and re-layouts  7.01 us
    all_to_all x1, waiting for transfers between devices, local(): lax.all_to_all(outcome, 'exp', split_axis=0, concat_axis=0, tiled=True)  6.97 us
    all_to_all x1, starting transfers between devices, local(): lax.all_to_all(outcome, 'exp', split_axis=0, concat_axis=0, tiled=True)  5.86 us
  transfers between devices with their start and end apart: 1, of which 1 were waited for; matrix products, arithmetic and copies ran while one was open for 0% of the time, Pallas kernels for 0%

profile of v2, /device:TPU:1, one launch (start us, length us, event | category | flops | bytes accessed | tf_op | source)
XLA Modules:
  0.0 227.5 jit_solution(9214609044014443544)
XLA Ops:
  0.0 0.7 copy-done
  0.7 0.1 constant_dynamic-slice_fusion
  0.8 0.1 copy.18
  0.9 0.1 eq.73
  1.0 0.1 fusion.9
  1.0 0.1 reduce_window_sum.11
  1.1 0.2 select_reduce_fusion
  2.0 0.7 broadcast_in_dim.6.attn_gain
  2.7 0.7 broadcast_in_dim.7.ffn_gain
  3.4 0.3 fusion.6
  3.7 0.1 pad_maximum_fusion
  3.8 0.0 copy-start.1
  3.8 1.2 copy-done.1
  5.0 0.9 copy-done.2
  6.0 0.9 copy-done.3
  6.9 0.8 copy-done.4
  7.8 0.8 copy-done.5
  8.6 0.8 copy-done.6
  9.4 0.8 copy-done.7
  10.1 83.8 %mixer.1 = (bf16[16,4096]{1,0:T(8,128)(2,1)S(1)}, bf16[16,4096]{1,0:T(8,128)(2,1)S(1)}) custom-call(bf16[128,4096]{1,0:T(8,128)(2,1)S(1)} %copy-done.1, bf16[1,4096]{1,0:T(2,128)(2,1)S(1)} %broadcast_in_dim.6.attn_gain, bf16[256,512]{1,0:T(8,128)(2,1)S(1)} %copy-done.2, bf16[256,128]{1,0:T(8,128)(2,1)S(1)} %copy-done.4, bf16[256,128]{1,0:T(8,128)(2,1)S(1)} %copy-done.5, ...), custom_call_target="tpu_custom_call" | custom-call | tf_op jit(solution)/shard_map/mixer/pallas_call | solution.py:626
  93.9 0.2 broadcast_in_dim.8
  94.1 0.1 reshape.105
  94.2 0.3 fusion
  94.6 14.9 %all_to_all.10 = bf16[8,8,4096]{2,1,0:T(8,128)(2,1)} all-to-all(bf16[8,8,4096]{2,1,0:T(8,128)(2,1)S(1)} %fusion), channel_id=1, replica_groups=mesh['ctx'=16,'exp'=8] {'exp'}, dimensions={0} | all-to-all | bytes 1048576 | tf_op jit(solution)/shard_map/all_to_all | solution.py:715
  109.4 104.1 %experts.1 = bf16[64,4096]{1,0:T(8,128)(2,1)} custom-call(bf16[64,4096]{1,0:T(8,128)(2,1)} %bitcast.13, bf16[1,4096,896]{2,1,0:T(8,128)(2,1)} %gate.1, bf16[1,4096,896]{2,1,0:T(8,128)(2,1)} %up.1, bf16[1,896,4096]{2,1,0:T(8,128)(2,1)} %down.1), custom_call_target="tpu_custom_call" | custom-call | tf_op jit(solution)/shard_map/experts/pallas_call | solution.py:381
  213.5 5.9 %all-to-all-start.1 = ((bf16[8,8,4096]{2,1,0:T(8,128)(2,1)}), bf16[8,8,4096]{2,1,0:T(8,128)(2,1)S(1)}, u32[]{:S(2)}, u32[]{:S(2)}) async-start(bf16[8,8,4096]{2,1,0:T(8,128)(2,1)} %bitcast.12), calls=%async_computation.1 | async-start | bytes 1048576 | tf_op jit(solution)/shard_map/all_to_all | solution.py:718
  219.4 0.1 eq.77
  219.4 0.1 copy.19
  219.5 7.0 %all-to-all-done.1 = bf16[8,8,4096]{2,1,0:T(8,128)(2,1)S(1)} async-done(((bf16[8,8,4096]{2,1,0:T(8,128)(2,1)}), bf16[8,8,4096]{2,1,0:T(8,128)(2,1)S(1)}, u32[]{:S(2)}, u32[]{:S(2)}) %all-to-all-start.1) | async-done | bytes 524320 | tf_op jit(solution)/shard_map/all_to_all | solution.py:718
  226.5 0.0 copy-done.8
  226.5 0.3 fusion.1
  226.8 0.7 add_convert_fusion
  (11 shorter events, 0.0 us)
Async XLA Ops:
  0.0 0.7 copy-start
  3.8 1.2 copy-start.1
  5.0 0.9 copy-start.2
  6.0 0.9 copy-start.3
  6.9 0.8 copy-start.4
  7.8 0.8 copy-start.5
  8.6 0.8 copy-start.6
  9.4 0.8 copy-start.7
  109.4 117.1 %copy-start.8 = (f32[16,2]{0,1:T(2,128)S(1)}, f32[16,2]{0,1:T(2,128)}, u32[]{:S(2)}) copy-start(f32[16,2]{0,1:T(2,128)} %param.29) | copy-start | bytes 388
  213.5 13.0 %all-to-all-start.1 = ((bf16[8,8,4096]{2,1,0:T(8,128)(2,1)}), bf16[8,8,4096]{2,1,0:T(8,128)(2,1)S(1)}, u32[]{:S(2)}, u32[]{:S(2)}) async-start(bf16[8,8,4096]{2,1,0:T(8,128)(2,1)} %bitcast.12), calls=%async_computation.1 | async-start | bytes 1048576 | tf_op jit(solution)/shard_map/all_to_all | solution.py:718

commit v3 on v2

--- a/solution.py
+++ b/solution.py
@@ -151,15 +151,9 @@
             self.copy(j, False).wait_send()
 
 
-CHUNKS = (((0, 0), (0, 1)), ((3, 0), (1, 0)), ((3, 1), (1, 1)), ((2, 0), (2, 1)))
-PLACE = {}
-for _g, _pair in enumerate(CHUNKS):
-    for _i, _xy in enumerate(_pair):
-        for _dk in range(2):
-            PLACE[_xy + (_dk,)] = (_g, _dk * 2 + _i)
+CHIPS = ((0, 0), (0, 1), (3, 0), (1, 0), (3, 1), (1, 1), (2, 1), (2, 0))
+SOURCE = {1: 0, 3: 1, 2: 2}
 ROWS = 64
-GU = 128
-DN = 512
 
 
 class LocalGather(Gather):
@@ -179,25 +173,23 @@
 
 
 def expert_kernel(
-    arrived, gate, up, down, out,
-    tok, wgu, wdn, hid, part, from_sib, from_x, from_y,
-    ag_send, ag_recv, w_sem, own_sem, rs_send, rs_recv,
+    arrived, gate, up, down, residual, mix, out,
+    tok, wgu, wdn, hid, part, from_sib, x_first, y_sum, y_first, x_sum, slots, returned,
+    ag_send, ag_recv, w_sem, own_sem, rs_send, rs_recv, back_send, back_recv,
 ):
-    e = lax.axis_index("exp")
-    units = gate.shape[2] // GU
-    width = down.shape[2]
+    c, e = lax.axis_index("ctx"), lax.axis_index("exp")
+    peers = [lax.rem(e + d, 8) for d in range(1, 8)]
+    f32, bf16 = jnp.float32, jnp.bfloat16
+    units, width = down.shape[1:]
+    half_width = width // 2
     own_copy = pltpu.make_async_copy(arrived, tok.at[0, pl.ds(0, ROWS), :], own_sem)
     own_copy.start()
-    loads = []
-    for j in range(units):
-        for s, w in enumerate((gate, up)):
-            loads.append(
-                pltpu.make_async_copy(
-                    w.at[0, :, pl.ds(j * GU, GU)], wgu.at[j, :, pl.ds(s * GU, GU)], w_sem.at[2 * j + s]
-                )
-            )
-    loads.append(pltpu.make_async_copy(down.at[0], wdn, w_sem.at[2 * units]))
-    greet(ctx_neighbours() + [(ctx_at((2, 0, 0)), e)])
+    loads = [
+        pltpu.make_async_copy(gate.at[0], wgu.at[:, pl.ds(0, units)], w_sem.at[0]),
+        pltpu.make_async_copy(up.at[0], wgu.at[:, pl.ds(units, units)], w_sem.at[1]),
+        pltpu.make_async_copy(down.at[0], wdn, w_sem.at[2]),
+    ]
+    greet(ctx_neighbours() + [(ctx_at((2, 0, 0)), e)] + [(c, to) for to in peers])
     own_copy.wait()
 
     pieces = []
@@ -205,15 +197,15 @@
         rows = ROWS // 2
 
         def slot(rel, half, first=number * rows, rows=rows):
-            g, place = PLACE[rel]
+            g, start = CHIPS.index(rel[:2]), rel[2] * ROWS + first
             if half is None:
-                return tok.at[g, pl.ds(place * ROWS + first, rows), :]
-            return tok.at[g, pl.ds(place * ROWS + first + half * (rows // 2), rows // 2), :]
+                return tok.at[g, pl.ds(start, rows), :]
+            return tok.at[g, pl.ds(start + half * (rows // 2), rows // 2), :]
 
         pieces.append(LocalGather(number, mode, slot, ag_send, ag_recv))
     first, second = pieces
-    for piece in pieces:
-        piece.start(None)
+    second.start(None)
+    first.start(None)
     for load in loads:
         load.start()
 
@@ -225,23 +217,6 @@
     def need(piece, *js):
         for j in js:
             piece.arrive(j)
-
-    def gate_up(g, lo, hi):
-        def body(j, _):
-            both = jnp.dot(tok[g], wgu[j], preferred_element_type=jnp.float32)
-            v = both[:, :GU]
-            hid[:, pl.ds(pl.multiple_of(j * GU, GU), GU)] = (v / (1.0 + jnp.exp(-v)) * both[:, GU:]).astype(jnp.bfloat16)
-            return 0
-
-        lax.fori_loop(lo, hi, body, 0)
-
-    def down_part(g, lo, hi):
-        def body(n, _):
-            cols = pl.ds(pl.multiple_of(n * DN, DN), DN)
-            part[g, :, cols] = jnp.dot(hid[...], wdn[:, cols], preferred_element_type=jnp.float32).astype(jnp.bfloat16)
-            return 0
-
-        lax.fori_loop(lo, hi, body, 0)
 
     def rs_copy(j, source, target, to):
         return pltpu.make_async_remote_copy(
@@ -249,167 +224,194 @@
             device_id=(ctx_at(to), e), device_id_type=MESH,
         )
 
-    half = 2 * ROWS
-    to_sib = [
-        rs_copy(g, part.at[g, pl.ds(half, half), :], from_sib.at[g], (0, 0, 1)) for g in range(4)
-    ]
-    near, far = pl.ds(0, ROWS), pl.ds(ROWS, ROWS)
-    to_x = {
-        1: [
-            rs_copy(4, part.at[1, near, :], from_x.at[0, 0], (-1, 0, 0)),
-            rs_copy(5, part.at[1, far, :], from_x.at[1, 0], (1, 0, 0)),
-        ],
-        2: [
-            rs_copy(6, part.at[2, near, :], from_x.at[0, 1], (-1, 0, 0)),
-            rs_copy(7, part.at[2, far, :], from_x.at[1, 1], (1, 0, 0)),
-        ],
-        3: [
-            rs_copy(8, part.at[3, far, :], from_x.at[2, 1], (2, 0, 0)),
-            rs_copy(9, part.at[3, near, :], from_x.at[2, 0], (2, 0, 0)),
-        ],
+    mine = pl.ds(0, ROWS)
+    lhs, rhs = pl.ds(0, half_width), pl.ds(half_width, half_width)
+
+    def to_sib(g):
+        return rs_copy(g, part.at[g, pl.ds(ROWS, ROWS), :], from_sib.at[g], (0, 0, 1))
+
+    x_first_copy, y_first_copy, x_sum_copy = {}, {}, {}
+    for g, (dx, dy) in enumerate(CHIPS):
+        if dx:
+            s = SOURCE[dx]
+            x_first_copy[dx, dy] = rs_copy(8 + s * 2 + dy, part.at[g, mine, lhs], x_first.at[s, dy], (dx, 0, 0))
+            if not dy:
+                x_sum_copy[dx] = rs_copy(14 + s, part.at[g, mine, rhs], x_sum.at[s], (dx, 0, 0))
+        if dy:
+            y_first_copy[dx] = rs_copy(17 + dx, part.at[g, mine, rhs], y_first.at[dx], (0, 1, 0))
+    y_sum_copy = rs_copy(21, part.at[1, mine, lhs], y_sum, (0, 1, 0))
+
+    def merge(g):
+        to_sib(g).wait_recv()
+        part[g, mine, :] = (part[g, mine, :].astype(f32) + from_sib[g].astype(f32)).astype(bf16)
+
+    def send(g):
+        dx, dy = CHIPS[g]
+        if dx:
+            x_first_copy[dx, dy].start()
+        if dy:
+            y_first_copy[dx].start()
+
+    def send_right(dx):
+        g = CHIPS.index((dx, 0))
+        y_first_copy[dx].wait_recv()
+        part[g, mine, rhs] = (part[g, mine, rhs].astype(f32) + y_first[dx].astype(f32)).astype(bf16)
+        if dx:
+            x_sum_copy[dx].start()
+
+    before = {
+        0: lambda: (need(first, 3), need(second, 3), loads[0].wait(), loads[1].wait()),
+        1: lambda: (
+            forward(second, 0, 1), need(first, 6), need(second, 10), forward(first, 1, 2),
+        ),
+        2: lambda: (forward(second, 4, 7), need(first, 8), need(second, 6)),
+        3: lambda: (forward(first, 4, 5), need(first, 10), need(second, 9)),
+        4: lambda: (forward(first, 7, 9), need(first, 12), need(second, 15)),
+        5: lambda: (forward(first, 11, 13), need(first, 14), need(second, 16)),
+        6: lambda: (need(first, 17, 18), need(second, 17, 18)),
+        7: lambda: (need(first, 15, 16), need(second, 12, 14)),
     }
-    to_y = rs_copy(10, part.at[0, far, :], from_y, (0, 1, 0))
-    tile = 16
-
-    def add_rows(rows, terms, store):
-        def body(i, _):
-            at = pl.multiple_of(i * tile, tile)
-            total = terms[0](at)
-            for term in terms[1:]:
-                total = total + term(at)
-            store(at, total.astype(jnp.bfloat16))
-            return 0
-
-        lax.fori_loop(0, rows // tile, body, 0)
-
-    def merge(g):
-        to_sib[g].wait_recv()
-
-        def store(at, value):
-            part[g, pl.ds(at, tile), :] = value
-
-        add_rows(
-            half,
-            [
-                lambda at: part[g, pl.ds(at, tile), :].astype(jnp.float32),
-                lambda at: from_sib[g, pl.ds(at, tile), :].astype(jnp.float32),
-            ],
-            store,
-        )
-        for copy in to_x.get(g, ()):
-            copy.start()
-
-    forward(first, 0)
-    forward(second, 2)
-    need(first, 3, 6)
-    need(second, 3, 10)
-    for load in loads[:-1]:
-        load.wait()
-    gate_up(0, 0, 4)
-    forward(first, 1, 2)
-    forward(second, 0, 1)
-    gate_up(0, 4, units)
-    loads[-1].wait()
-    forward(first, 4, 5)
-    down_part(0, 0, width // DN)
-    to_sib[0].start()
-    forward(second, 4, 7)
-    forward(second, 5, 8)
-    need(first, 8, 10)
-    need(second, 6, 9)
-    gate_up(1, 0, 4)
-    forward(first, 7, 9)
-    gate_up(1, 4, units)
-    forward(second, 11, 13)
-    down_part(1, 0, width // DN)
-    to_sib[1].start()
-    merge(0)
-    forward(first, 11, 13)
-    need(first, 12, 14)
-    need(second, 15, 16)
-    gate_up(2, 0, units)
-    merge(1)
-    down_part(2, 0, width // DN)
-    to_sib[2].start()
-    need(first, 15, 16, 17, 18)
-    need(second, 12, 14, 17, 18)
-    gate_up(3, 0, units)
-    merge(2)
-    down_part(3, 0, width // DN)
-    to_sib[3].start()
-    merge(3)
-
-    to_x[2][0].wait_recv()
-    to_x[2][1].wait_recv()
-    to_x[3][0].wait_recv()
-
-    def store_far(at, value):
-        part[0, pl.ds(ROWS + at, tile), :] = value
-
-    add_rows(
-        ROWS,
-        [lambda at: part[0, pl.ds(ROWS + at, tile), :].astype(jnp.float32)]
-        + [lambda at, s=s: from_x[s, 1, pl.ds(at, tile), :].astype(jnp.float32) for s in range(3)],
-        store_far,
-    )
-    to_y.start()
-    to_x[1][0].wait_recv()
-    to_x[1][1].wait_recv()
-    to_x[3][1].wait_recv()
-    to_y.wait_recv()
-
-    def store_out(at, value):
-        out[pl.ds(at, tile), :] = value
-
-    add_rows(
-        ROWS,
-        [lambda at: part[0, pl.ds(at, tile), :].astype(jnp.float32)]
-        + [lambda at, s=s: from_x[s, 0, pl.ds(at, tile), :].astype(jnp.float32) for s in range(3)]
-        + [lambda at: from_y[pl.ds(at, tile), :].astype(jnp.float32)],
-        store_out,
-    )
+    between = {
+        0: lambda: (forward(first, 0), forward(second, 2), loads[2].wait()),
+        3: lambda: (forward(second, 5, 8), send_right(0)),
+        5: lambda: (forward(second, 11, 13),),
+        6: lambda: (send_right(3),),
+        7: lambda: (send_right(1),),
+    }
+
+    def at_step(g, actions):
+        for at, action in actions.items():
+
+            @pl.when(g == at)
+            def _(action=action):
+                action()
+
+    def step(g, _):
+        at_step(g, before)
+        both = jnp.dot(tok[g], wgu[...], preferred_element_type=f32)
+        v = both[:, :units]
+        hid[...] = (v / (1.0 + jnp.exp(-v)) * both[:, units:]).astype(bf16)
+
+        @pl.when(g > 0)
+        def _():
+            merge(g - 1)
+
+        for at in range(1, 8):
+            pl.when(g == at)(functools.partial(send, at - 1))
+        at_step(g, between)
+        part[g] = jnp.dot(hid[...], wdn[...], preferred_element_type=f32).astype(bf16)
+        to_sib(g).start()
+        return 0
+
+    lax.fori_loop(0, 8, step, 0)
+    merge(7)
+    send(7)
+    send_right(2)
+
+    moves = {}
+
+    def give_back(h, value):
+        cols = rhs if h else lhs
+        slots[:, :, cols] = value.reshape(8, ROWS // 8, half_width).astype(bf16)
+        moves[h] = [
+            pltpu.make_async_remote_copy(
+                src_ref=slots.at[to, :, cols],
+                dst_ref=returned.at[e, :, cols],
+                send_sem=back_send.at[h, d],
+                recv_sem=back_recv.at[h, d],
+                device_id=(c, to),
+                device_id_type=MESH,
+            )
+            for d, to in enumerate(peers)
+        ]
+        for move in moves[h]:
+            move.start()
+        returned[e, :, cols] = slots[e, :, cols]
+
+    for dx in (1, 3, 2):
+        x_first_copy[dx, 1].wait_recv()
+    total = part[1, mine, lhs].astype(f32)
+    for s in range(3):
+        total = total + x_first[s, 1].astype(f32)
+    part[1, mine, lhs] = total.astype(bf16)
+    y_sum_copy.start()
+    for dx in (1, 3, 2):
+        x_sum_copy[dx].wait_recv()
+    total = part[0, mine, rhs].astype(f32)
+    for s in range(3):
+        total = total + x_sum[s].astype(f32)
+    give_back(1, total)
+    for dx in (1, 3, 2):
+        x_first_copy[dx, 0].wait_recv()
+    total = part[0, mine, lhs].astype(f32)
+    for s in range(3):
+        total = total + x_first[s, 0].astype(f32)
+    y_sum_copy.wait_recv()
+    give_back(0, total + y_sum[...].astype(f32))
+    hi = mix[...].astype(bf16)
+    lo = (mix[...] - hi.astype(f32)).astype(bf16)
+    for h, cols in ((1, rhs), (0, lhs)):
+        for move in moves[h]:
+            move.wait_recv()
+        outcome = returned[:, :, cols].astype(f32).reshape(ROWS, half_width).astype(bf16)
+        mixture = jnp.dot(hi, outcome, preferred_element_type=f32) + jnp.dot(lo, outcome, preferred_element_type=f32)
+        out[:, cols] = (residual[:, cols].astype(f32) + mixture).astype(bf16)
+    for h in range(2):
+        for move in moves[h]:
+            move.wait_send()
     for piece in pieces:
         piece.drain()
-    for copy in to_sib + to_x[1] + to_x[2] + to_x[3] + [to_y]:
-        copy.wait_send()
-
-
-def experts(arrived, w_gate, w_up, w_down):
+    for copies in (x_first_copy, y_first_copy, x_sum_copy):
+        for copy in copies.values():
+            copy.wait_send()
+    y_sum_copy.wait_send()
+    for g in range(8):
+        to_sib(g).wait_send()
+
+
+def experts(arrived, w_gate, w_up, w_down, residual, mix):
     rows, width = arrived.shape
     ff = w_gate.shape[2]
     bf16 = jnp.bfloat16
     return pl.pallas_call(
         expert_kernel,
-        out_shape=jax.ShapeDtypeStruct((rows, width), bf16),
-        in_specs=[pl.BlockSpec(memory_space=pl.ANY)] * 4,
+        out_shape=jax.ShapeDtypeStruct(residual.shape, bf16),
+        in_specs=[pl.BlockSpec(memory_space=pltpu.HBM)] * 4 + [pl.BlockSpec(memory_space=pltpu.VMEM)] * 2,
         out_specs=pl.BlockSpec(memory_space=pltpu.VMEM),
         scratch_shapes=[
-            pltpu.VMEM((4, 4 * rows, width), bf16),
-            pltpu.VMEM((ff // GU, width, 2 * GU), bf16),
+            pltpu.VMEM((8, 2 * rows, width), bf16),
+            pltpu.VMEM((width, 2 * ff), bf16),
             pltpu.VMEM((ff, width), bf16),
-            pltpu.VMEM((4 * rows, ff), bf16),
-            pltpu.VMEM((4, 4 * rows, width), bf16),
-            pltpu.VMEM((4, 2 * rows, width), bf16),
-            pltpu.VMEM((3, 2, rows, width), bf16),
-            pltpu.VMEM((rows, width), bf16),
+            pltpu.VMEM((2 * rows, ff), bf16),
+            pltpu.VMEM((8, 2 * rows, width), bf16),
+            pltpu.VMEM((8, rows, width), bf16),
+            pltpu.VMEM((3, 2, rows, width // 2), bf16),
+            pltpu.VMEM((rows, width // 2), bf16),
+            pltpu.VMEM((4, rows, width // 2), bf16),
+            pltpu.VMEM((3, rows, width // 2), bf16),
+            pltpu.VMEM((8, rows // 8, width), bf16),
+            pltpu.VMEM((8, rows // 8, width), bf16),
             pltpu.SemaphoreType.DMA((2, N_TRANSFERS)),
             pltpu.SemaphoreType.DMA((2, N_TRANSFERS)),
-            pltpu.SemaphoreType.DMA((2 * (ff // GU) + 1,)),
+            pltpu.SemaphoreType.DMA((3,)),
             pltpu.SemaphoreType.DMA,
-            pltpu.SemaphoreType.DMA((11,)),
-            pltpu.SemaphoreType.DMA((11,)),
+            pltpu.SemaphoreType.DMA((22,)),
+            pltpu.SemaphoreType.DMA((22,)),
+            pltpu.SemaphoreType.DMA((2, 7)),
+            pltpu.SemaphoreType.DMA((2, 7)),
         ],
         compiler_params=pltpu.CompilerParams(
-            collective_id=3, has_side_effects=True, vmem_limit_bytes=56 * 1024 * 1024
+            collective_id=3, has_side_effects=True, vmem_limit_bytes=58 * 1024 * 1024
         ),
         name="experts",
-    )(arrived, w_gate, w_up, w_down)
+    )(arrived, w_gate, w_up, w_down, residual, mix)
+
 
 def mixer_kernel(
-    hidden, attn_gain, w_query, w_key, w_value, w_out, prior_keys, prior_values, cosine, sine, ffn_gain,
-    residual_out, normed_out,
-    normed, wkv, wq, kv, wo, query, scores, best, mass, blend, attended, part, from_exp,
-    send, recv, local, rs_send, rs_recv,
+    hidden, attn_gain, w_query, w_key, w_value, w_out, prior_keys, prior_values, cosine, sine, ffn_gain, select,
+    residual_out, arrived_out,
+    normed, wkv, wq, kv, wo, query, scores, best, mass, blend, attended, part, from_exp, slots,
+    send, recv, local, rs_send, rs_recv, to_send, to_recv,
 ):
     c, e = lax.axis_index("ctx"), lax.axis_index("exp")
     f32, bf16 = jnp.float32, jnp.bfloat16
@@ -567,39 +569,53 @@
         (1.5, 0, normalise),
         (4.5, 0, keys_and_values),
         (7.5, 0, forward_now),
-        (8.5, 0, queries),
-        (8.6, 0, all_scores),
-        (9.5, 0, blended),
+        (8.05, 0, queries),
+        (8.1, 0, all_scores),
+        (8.6, 0, blended),
+    ]
+    peers = [lax.rem(e + d, 8) for d in range(1, 8)]
+    plane = 4 * out_cols
+    shares = {}
+
+    def project(dx, wants):
+        for piece, js in zip(pieces[6:], wants):
+            for j in js:
+                piece.arrive(j)
+        x = lax.rem(c // 4 + dx, NX)
+
+        def one(i, _):
+            index = x * 4 + i
+            cols = pl.ds(pl.multiple_of(index * out_cols, out_cols), out_cols)
+            part[:, cols] = jnp.dot(attended[...], wo[index], preferred_element_type=f32).astype(bf16)
+            return 0
+
+        lax.fori_loop(0, 4, one, 0)
+        cols = pl.ds(pl.multiple_of(x * plane, plane), plane)
+        shares[dx] = [
+            pltpu.make_async_remote_copy(
+                src_ref=part.at[pl.ds(pl.multiple_of(to * tok_dev, tok_dev), tok_dev), cols],
+                dst_ref=from_exp.at[d, :, cols],
+                send_sem=rs_send.at[dx, d],
+                recv_sem=rs_recv.at[dx, d],
+                device_id=(c, to),
+                device_id_type=MESH,
+            )
+            for d, to in enumerate(peers)
+        ]
+        for share in shares[dx]:
+            share.start()
+
+    timeline += [
+        (9.1, 0, lambda: project(0, ((3, 6), (3, 10)))),
+        (9.2, 0, lambda: project(3, ((8, 12), (6, 15)))),
+        (9.3, 0, lambda: project(1, ((10, 14), (9, 16)))),
+        (11.0, 0, lambda: project(2, ((15, 16, 17, 18), (12, 14, 17, 18)))),
     ]
     for _, _, action in sorted(timeline, key=lambda item: item[:2]):
         action()
-    for piece in pieces[6:]:
-        piece.finish()
-
-    def project(i, _):
-        cols = pl.ds(pl.multiple_of(i * out_cols, out_cols), out_cols)
-        part[:, cols] = jnp.dot(attended[...], wo[i], preferred_element_type=f32).astype(bf16)
-        return 0
-
-    lax.fori_loop(0, width // out_cols, project, 0)
-
-    shares = []
-    for d in range(1, 8):
-        to = lax.rem(e + d, 8)
-        shares.append(
-            pltpu.make_async_remote_copy(
-                src_ref=part.at[pl.ds(pl.multiple_of(to * tok_dev, tok_dev), tok_dev), :],
-                dst_ref=from_exp.at[d - 1],
-                send_sem=rs_send.at[d - 1],
-                recv_sem=rs_recv.at[d - 1],
-                device_id=(c, to),
-                device_id_type=MESH,
-            )
-        )
-    for share in shares:
-        share.start()
-    for share in shares:
-        share.wait_recv()
+    for dx in (0, 3, 1, 2):
+        for share in shares[dx]:
+            share.wait_recv()
     mine = pl.ds(pl.multiple_of(e * tok_dev, tok_dev), tok_dev)
     total = part[mine, :].astype(f32)
     for d in range(7):
@@ -608,25 +624,49 @@
     residual_out[...] = residual
     wide = residual.astype(f32)
     inverse = lax.rsqrt(jnp.mean(wide * wide, axis=-1, keepdims=True) + 1e-05)
-    normed_out[...] = (wide * inverse * ffn_gain[...].astype(f32)).astype(bf16)
+    ready = (wide * inverse * ffn_gain[...].astype(f32)).astype(bf16)
+    chosen = jnp.dot(select[...], ready, preferred_element_type=f32)
+    slots[...] = chosen.reshape(slots.shape).astype(bf16)
+    moves = [
+        pltpu.make_async_remote_copy(
+            src_ref=slots.at[to],
+            dst_ref=arrived_out.at[e],
+            send_sem=to_send.at[d],
+            recv_sem=to_recv.at[d],
+            device_id=(c, to),
+            device_id_type=MESH,
+        )
+        for d, to in enumerate(peers)
+    ]
+    for move in moves:
+        move.start()
+    arrived_out[e] = slots[e]
     for piece in pieces + [now]:
         piece.drain()
-    for share in shares:
-        share.wait_send()
-
-
-def mixer(hidden, attn_gain, w_query, w_key, w_value, w_out, prior_keys, prior_values, cosine, sine, ffn_gain):
+    for dx in (0, 3, 1, 2):
+        for share in shares[dx]:
+            share.wait_send()
+    for move in moves:
+        move.wait_send()
+    for move in moves:
+        move.wait_recv()
+
+
+def mixer(hidden, attn_gain, w_query, w_key, w_value, w_out, prior_keys, prior_values, cosine, sine, ffn_gain, select):
     tokens, width = hidden.shape
     depth, q_cols = w_query.shape
     bf16, f32 = jnp.bfloat16, jnp.float32
     span = 16 * tokens
     count = q_cols // HEAD_DIM * tokens
     vmem = pl.BlockSpec(memory_space=pltpu.VMEM)
-    anywhere = pl.BlockSpec(memory_space=pl.ANY)
+    anywhere = pl.BlockSpec(memory_space=pltpu.HBM)
     return pl.pallas_call(
         mixer_kernel,
-        out_shape=[jax.ShapeDtypeStruct((tokens // 8, width), bf16)] * 2,
-        in_specs=[vmem, vmem] + [anywhere] * 6 + [vmem] * 3,
+        out_shape=[
+            jax.ShapeDtypeStruct((tokens // 8, width), bf16),
+            jax.ShapeDtypeStruct((8, select.shape[0] // 8, width), bf16),
+        ],
+        in_specs=[vmem, vmem] + [anywhere] * 6 + [vmem] * 4,
         out_specs=[vmem] * 2,
         scratch_shapes=[
             pltpu.VMEM((tokens, width), bf16),
@@ -642,17 +682,20 @@
             pltpu.VMEM((tokens, q_cols), bf16),
             pltpu.VMEM((tokens, width), bf16),
             pltpu.VMEM((7, tokens // 8, width), bf16),
+            pltpu.VMEM((8, select.shape[0] // 8, width), bf16),
             pltpu.SemaphoreType.DMA((9, N_TRANSFERS)),
             pltpu.SemaphoreType.DMA((9, N_TRANSFERS)),
             pltpu.SemaphoreType.DMA((6,)),
+            pltpu.SemaphoreType.DMA((4, 7)),
+            pltpu.SemaphoreType.DMA((4, 7)),
             pltpu.SemaphoreType.DMA((7,)),
             pltpu.SemaphoreType.DMA((7,)),
         ],
         compiler_params=pltpu.CompilerParams(
-            collective_id=0, has_side_effects=True, vmem_limit_bytes=48 * 1024 * 1024
+            collective_id=0, has_side_effects=True, vmem_limit_bytes=60 * 1024 * 1024
         ),
         name="mixer",
-    )(hidden, attn_gain, w_query, w_key, w_value, w_out, prior_keys, prior_values, cosine, sine, ffn_gain)
+    )(hidden, attn_gain, w_query, w_key, w_value, w_out, prior_keys, prior_values, cosine, sine, ffn_gain, select)
 
 
 def local(
@@ -682,7 +725,18 @@
     frequency = jnp.exp(jnp.arange(half_dim).astype(jnp.float32) * (-2.0 * math.log(1000000.0) / HEAD_DIM))
     angles = positions.astype(jnp.float32)[:, None] * frequency[None, :]
     cosine, sine = jnp.cos(angles), jnp.sin(angles)
-    residual, normed_ffn = mixer(
+    capacity = 4 * tok_dev // exp_count
+    device_row = (ctx_index * exp_count + exp_index) * tok_dev
+    my_ids = lax.dynamic_slice_in_dim(expert_ids, device_row, tok_dev, 0)
+    flat = my_ids.reshape(-1)
+    same = flat[:, None] == flat[None, :]
+    earlier = jnp.arange(2 * tok_dev)[:, None] < jnp.arange(2 * tok_dev)[None, :]
+    place = flat * capacity + jnp.sum(same & earlier, axis=0, dtype=jnp.int32)
+    place = place.reshape(tok_dev, 2)
+    held = place[:, :, None] == jnp.arange(exp_count * capacity, dtype=jnp.int32)[None, None, :]
+    select = jnp.any(held, axis=1).T.astype(jnp.bfloat16)
+    mix = jnp.sum(jnp.where(held, gate_weights[:, :, None], 0.0), axis=1)
+    residual, arrived = mixer(
         hidden_in,
         attn_gain[None],
         w_query,
@@ -694,36 +748,9 @@
         jnp.concatenate([cosine, cosine], axis=1),
         jnp.concatenate([-sine, sine], axis=1),
         ffn_gain[None],
+        select,
     )
-    capacity = 4 * tok_dev // exp_count
-    device_row = (ctx_index * exp_count + exp_index) * tok_dev
-    my_ids = lax.dynamic_slice_in_dim(expert_ids, device_row, tok_dev, 0).reshape(-1)
-    onehot = (my_ids[:, None] == jnp.arange(exp_count, dtype=jnp.int32)[None, :]).astype(jnp.int32)
-    before = jnp.cumsum(onehot, axis=0) - onehot
-    slot_of = jnp.sum(before * onehot, axis=1)
-    slot_ids = jnp.arange(exp_count * capacity, dtype=jnp.int32)
-    select = (
-        (slot_ids[:, None] // capacity == my_ids[None, :])
-        & (slot_ids[:, None] % capacity == slot_of[None, :])
-    ).astype(jnp.bfloat16)
-    repeated = jnp.repeat(normed_ffn, 2, axis=0)
-    outgoing = (
-        jnp.dot(select, repeated, preferred_element_type=jnp.float32)
-        .astype(jnp.bfloat16)
-        .reshape(exp_count, capacity, model_width)
-    )
-    arrived = lax.all_to_all(outgoing, "exp", split_axis=0, concat_axis=0, tiled=True)
-    own_slots = experts(arrived.reshape(-1, model_width), w_gate, w_up, w_down)
-    outcome = own_slots.reshape(exp_count, capacity, model_width)
-    returned = lax.all_to_all(outcome, "exp", split_axis=0, concat_axis=0, tiled=True)
-    gathered_back = jnp.dot(
-        select.T,
-        returned.reshape(exp_count * capacity, model_width),
-        preferred_element_type=jnp.float32,
-    )
-    picked = gathered_back.reshape(tok_dev, 2, model_width)
-    mixture = jnp.sum(gate_weights[:, :, None] * picked, axis=1)
-    return (residual.astype(jnp.float32) + mixture).astype(jnp.bfloat16)
+    return experts(arrived.reshape(-1, model_width), w_gate, w_up, w_down, residual, mix)
 
 
 def solution(mesh):

time: 228 us -> 195 us (0.86)
  blocking collectives: 14.9 us -> 0 us
  waiting for transfers between devices: 6.97 us -> 0 us
  starting transfers between devices: 5.86 us -> 0 us
  local copies, waits for them, and re-layouts: 9.13 us -> 5.99 us
  Pallas kernels: 188 us -> 185 us
    all_to_all x1 -> x0, blocking collectives: 14.9 us -> none  [local(): lax.all_to_all(outgoing, 'exp', split_axis=0, concat_axis=0, tiled=True)]
    all_to_all x1 -> x0, waiting for transfers between devices: 6.97 us -> none  [local(): lax.all_to_all(outcome, 'exp', split_axis=0, concat_axis=0, tiled=True)]
    all_to_all x1 -> x0, starting transfers between devices: 5.86 us -> none  [local(): lax.all_to_all(outcome, 'exp', split_axis=0, concat_axis=0, tiled=True)]
    pallas_call x1, Pallas kernels: 104 us -> 99.3 us  [experts(): pl.pallas_call(expert_kernel, out_shape=jax.ShapeDtypeStruct(residual.sha...]
    unnamed x18 -> x4, local copies, waits for them, and re-layouts: 7.01 us -> 2.37 us
    pallas_call x1, Pallas kernels: 83.8 us -> 86.1 us  [mixer(): pl.pallas_call(mixer_kernel, out_shape=[jax.ShapeDtypeStruct((tokens // 8...]
  transfers between devices with their start and end apart: 1 -> 0, of which waited for: 1 -> 0; matrix products, arithmetic and copies ran while one was open for 0% -> 0% of each run, Pallas kernels for 0% -> 0%
where the time goes in v3:
time: 195 us
  Pallas kernels  185 us (95%)
  local copies, waits for them, and re-layouts  5.99 us (3%)
  other arithmetic  2.61 us (1%)
    pallas_call x1, Pallas kernels, experts(): pl.pallas_call(expert_kernel, out_shape=jax.ShapeDtypeStruct(residual.sha...  99.3 us
    pallas_call x1, Pallas kernels, mixer(): pl.pallas_call(mixer_kernel, out_shape=[jax.ShapeDtypeStruct((tokens // 8...  86.1 us

profile of v3, /device:TPU:1, one launch (start us, length us, event | category | flops | bytes accessed | tf_op | source)
XLA Modules:
  0.0 194.8 jit_solution(17174390417209415288)
XLA Ops:
  0.0 0.0 copy-start
  0.0 0.7 copy-done
  0.7 0.1 constant_dynamic-slice_fusion
  0.8 0.1 copy.26
  0.9 0.1 eq.28
  1.0 0.1 convert_reduce_fusion
  1.1 0.1 reduce_sum.21
  1.2 0.1 copy.24
  1.2 0.1 fusion.1
  1.3 0.7 copy.25
  2.7 0.3 fusion
  3.0 0.7 pad_maximum_fusion
  3.8 1.3 broadcast_in_dim.24.attn_gain
  5.1 1.3 broadcast_in_dim.25.ffn_gain
  6.4 86.1 %mixer.1 = (bf16[16,4096]{1,0:T(8,128)(2,1)}, bf16[8,8,4096]{2,1,0:T(8,128)(2,1)}) custom-call(bf16[128,4096]{1,0:T(8,128)(2,1)} %hidden.1, bf16[1,4096]{1,0:T(2,128)(2,1)} %broadcast_in_dim.24.attn_gain, bf16[256,512]{1,0:T(8,128)(2,1)} %w_query.1, bf16[256,128]{1,0:T(8,128)(2,1)} %w_key.1, bf16[256,128]{1,0:T(8,128)(2,1)} %w_value.1, ...), custom_call_target="tpu_custom_call" | custom-call | tf_op jit(solution)/shard_map/mixer/pallas_call | solution.py:663
  92.5 1.4 select_reduce_fusion.mix
  93.8 99.3 %experts.1 = bf16[16,4096]{1,0:T(8,128)(2,1)} custom-call(bf16[64,4096]{1,0:T(8,128)(2,1)} %bitcast.4, bf16[1,4096,896]{2,1,0:T(8,128)(2,1)} %gate.1, bf16[1,4096,896]{2,1,0:T(8,128)(2,1)} %up.1, bf16[1,896,4096]{2,1,0:T(8,128)(2,1)} %down.1, bf16[16,4096]{1,0:T(8,128)(2,1)} %get-tuple-element.8.residual, f32[16,64]{1,0:T(8,128)} %select_reduce_fusion.mix), custom_call_target="tpu_custom_call" | custom-call | tf_op jit(solution)/shard_map/experts/pallas_call | solution.py:376
  193.2 1.6 copy.29
  (4 shorter events, 0.0 us)
Async XLA Ops:
  0.0 0.7 copy-start

commit v4 on v3

--- a/solution.py
+++ b/solution.py
@@ -154,6 +154,7 @@
 CHIPS = ((0, 0), (0, 1), (3, 0), (1, 0), (3, 1), (1, 1), (2, 1), (2, 0))
 SOURCE = {1: 0, 3: 1, 2: 2}
 ROWS = 64
+PIECES = ((X_THEN_Y, 16), (Y_THEN_X, 48))
 
 
 class LocalGather(Gather):
@@ -192,31 +193,33 @@
     greet(ctx_neighbours() + [(ctx_at((2, 0, 0)), e)] + [(c, to) for to in peers])
     own_copy.wait()
 
-    pieces = []
-    for number, mode in enumerate((Y_THEN_X, X_THEN_Y)):
-        rows = ROWS // 2
-
-        def slot(rel, half, first=number * rows, rows=rows):
-            g, start = CHIPS.index(rel[:2]), rel[2] * ROWS + first
+    pieces, first, second, begin = [], [], [], 0
+    for number, (mode, rows) in enumerate(PIECES):
+
+        def slot(rel, half, begin=begin, rows=rows):
+            g, start = CHIPS.index(rel[:2]), rel[2] * ROWS + begin
             if half is None:
                 return tok.at[g, pl.ds(start, rows), :]
-            return tok.at[g, pl.ds(start + half * (rows // 2), rows // 2), :]
+            return tok.at[g, pl.ds(start, rows), pl.ds(half * half_width, half_width)]
 
         pieces.append(LocalGather(number, mode, slot, ag_send, ag_recv))
-    first, second = pieces
-    second.start(None)
-    first.start(None)
+        (first if mode is Y_THEN_X else second).append(pieces[-1])
+        begin += rows
+    for piece in pieces:
+        piece.start(None)
     for load in loads:
         load.start()
 
-    def forward(piece, *js):
+    def forward(group, *js):
         for j in js:
-            piece.arrive(j)
-            piece.start(j)
-
-    def need(piece, *js):
+            for piece in group:
+                piece.arrive(j)
+                piece.start(j)
+
+    def need(group, *js):
         for j in js:
-            piece.arrive(j)
+            for piece in group:
+                piece.arrive(j)
 
     def rs_copy(j, source, target, to):
         return pltpu.make_async_remote_copy(
@@ -260,9 +263,11 @@
             x_sum_copy[dx].start()
 
     before = {
-        0: lambda: (need(first, 3), need(second, 3), loads[0].wait(), loads[1].wait()),
+        0: lambda: (
+            forward(second, 2), forward(first, 0), need(first, 3), need(second, 3), loads[0].wait(), loads[1].wait(),
+        ),
         1: lambda: (
-            forward(second, 0, 1), need(first, 6), need(second, 10), forward(first, 1, 2),
+            need(first, 6), need(second, 10), forward(first, 1, 2),
         ),
         2: lambda: (forward(second, 4, 7), need(first, 8), need(second, 6)),
         3: lambda: (forward(first, 4, 5), need(first, 10), need(second, 9)),
@@ -272,7 +277,7 @@
         7: lambda: (need(first, 15, 16), need(second, 12, 14)),
     }
     between = {
-        0: lambda: (forward(first, 0), forward(second, 2), loads[2].wait()),
+        0: lambda: (forward(second, 0, 1), loads[2].wait()),
         3: lambda: (forward(second, 5, 8), send_right(0)),
         5: lambda: (forward(second, 11, 13),),
         6: lambda: (send_right(3),),
@@ -391,8 +396,8 @@
             pltpu.VMEM((3, rows, width // 2), bf16),
             pltpu.VMEM((8, rows // 8, width), bf16),
             pltpu.VMEM((8, rows // 8, width), bf16),
-            pltpu.SemaphoreType.DMA((2, N_TRANSFERS)),
-            pltpu.SemaphoreType.DMA((2, N_TRANSFERS)),
+            pltpu.SemaphoreType.DMA((len(PIECES), N_TRANSFERS)),
+            pltpu.SemaphoreType.DMA((len(PIECES), N_TRANSFERS)),
             pltpu.SemaphoreType.DMA((3,)),
             pltpu.SemaphoreType.DMA,
             pltpu.SemaphoreType.DMA((22,)),
@@ -434,7 +439,7 @@
                 (prior_keys, kv.at[own_keys, left]),
                 (prior_values, kv.at[own_keys, right]),
                 (w_query, wq.at[own_rows, :]),
-                (w_out, wo.at[c]),
+                (w_out, wo.at[:, pl.ds(pl.multiple_of(c * out_cols, out_cols), out_cols)]),
             )
         )
     ]
@@ -457,7 +462,10 @@
     def block_of(buffer, first, rows):
         def slot(index, half):
             part_rows = rows if half is None else rows // 2
-            return buffer.at[index, pl.ds(first + (0 if half is None else half * part_rows), part_rows), :]
+            return buffer.at[
+                pl.ds(first + (0 if half is None else half * part_rows), part_rows),
+                pl.ds(pl.multiple_of(index * out_cols, out_cols), out_cols),
+            ]
 
         return slot
 
@@ -477,7 +485,7 @@
         rows = pl.ds(pl.multiple_of(i * tile, tile), tile)
         wide = hidden[rows, :].astype(f32)
         inverse = lax.rsqrt(jnp.mean(wide * wide, axis=-1, keepdims=True) + 1e-05)
-        normed[rows, :] = (wide * inverse * attn_gain[...].astype(f32)).astype(bf16)
+        normed[rows, :] = (wide * inverse * attn_gain[...].astype(f32)[None]).astype(bf16)
         return 0
 
     def normalise():
@@ -498,9 +506,9 @@
     def queries():
         for piece in pieces[4:6]:
             piece.finish()
+        raw = jnp.dot(normed[...], wq[...], preferred_element_type=f32)
         for g in range(heads):
-            raw = jnp.dot(normed[...], wq[:, pl.ds(g * HEAD_DIM, HEAD_DIM)], preferred_element_type=f32)
-            query[pl.ds(g * tokens, tokens), :] = turned(raw)
+            query[pl.ds(g * tokens, tokens), :] = turned(raw[:, g * HEAD_DIM:(g + 1) * HEAD_DIM])
 
     count = heads * tokens
     block = 2 * tokens
@@ -583,14 +591,8 @@
                 piece.arrive(j)
         x = lax.rem(c // 4 + dx, NX)
 
-        def one(i, _):
-            index = x * 4 + i
-            cols = pl.ds(pl.multiple_of(index * out_cols, out_cols), out_cols)
-            part[:, cols] = jnp.dot(attended[...], wo[index], preferred_element_type=f32).astype(bf16)
-            return 0
-
-        lax.fori_loop(0, 4, one, 0)
         cols = pl.ds(pl.multiple_of(x * plane, plane), plane)
+        part[:, cols] = jnp.dot(attended[...], wo[:, cols], preferred_element_type=f32).astype(bf16)
         shares[dx] = [
             pltpu.make_async_remote_copy(
                 src_ref=part.at[pl.ds(pl.multiple_of(to * tok_dev, tok_dev), tok_dev), cols],
@@ -624,7 +626,7 @@
     residual_out[...] = residual
     wide = residual.astype(f32)
     inverse = lax.rsqrt(jnp.mean(wide * wide, axis=-1, keepdims=True) + 1e-05)
-    ready = (wide * inverse * ffn_gain[...].astype(f32)).astype(bf16)
+    ready = (wide * inverse * ffn_gain[...].astype(f32)[None]).astype(bf16)
     chosen = jnp.dot(select[...], ready, preferred_element_type=f32)
     slots[...] = chosen.reshape(slots.shape).astype(bf16)
     moves = [
@@ -673,7 +675,7 @@
             pltpu.VMEM((16 * depth, 2 * HEAD_DIM), bf16),
             pltpu.VMEM((16 * depth, q_cols), bf16),
             pltpu.VMEM((2 * span, 2 * HEAD_DIM), bf16),
-            pltpu.VMEM((16,) + w_out.shape, bf16),
+            pltpu.VMEM((w_out.shape[0], width), bf16),
             pltpu.VMEM((count, HEAD_DIM), bf16),
             pltpu.VMEM((count, span + tokens), f32),
             pltpu.VMEM((count, tokens), f32),
@@ -738,7 +740,7 @@
     mix = jnp.sum(jnp.where(held, gate_weights[:, :, None], 0.0), axis=1)
     residual, arrived = mixer(
         hidden_in,
-        attn_gain[None],
+        attn_gain,
         w_query,
         w_key,
         w_value,
@@ -747,7 +749,7 @@
         prior_values,
         jnp.concatenate([cosine, cosine], axis=1),
         jnp.concatenate([-sine, sine], axis=1),
-        ffn_gain[None],
+        ffn_gain,
         select,
     )
     return experts(arrived.reshape(-1, model_width), w_gate, w_up, w_down, residual, mix)

time: 195 us -> 188 us (0.964)
  Pallas kernels: 185 us -> 180 us
  local copies, waits for them, and re-layouts: 5.99 us -> 3.39 us
    pallas_call x1, Pallas kernels: 99.3 us -> 94.8 us  [experts(): pl.pallas_call(expert_kernel, out_shape=jax.ShapeDtypeStruct(residual.sha...]
    broadcast_in_dim x2 -> x0, local copies, waits for them, and re-layouts: 2.6 us -> none  [the longest x1 1.3 us: local(): ffn_gain[None]]
where the time goes in v4:
time: 188 us; the launch traced here: 187 us
  Pallas kernels  180 us (96%)
  local copies, waits for them, and re-layouts  3.39 us (2%)
  other arithmetic  2.61 us (1%)
    pallas_call x1, Pallas kernels, experts(): pl.pallas_call(expert_kernel, out_shape=jax.ShapeDtypeStruct(residual.sha...  94.8 us
    pallas_call x1, Pallas kernels, mixer(): pl.pallas_call(mixer_kernel, out_shape=[jax.ShapeDtypeStruct((tokens // 8...  85.3 us

profile of v4, /device:TPU:1, one launch (start us, length us, event | category | flops | bytes accessed | tf_op | source)
XLA Modules:
  0.0 186.8 jit_solution(10922109524880192777)
XLA Ops:
  0.0 0.0 copy-start
  0.0 0.7 copy-done
  0.7 0.1 constant_dynamic-slice_fusion
  0.8 0.1 copy.26
  0.9 0.1 eq.28
  1.0 0.1 convert_reduce_fusion
  1.1 0.1 reduce_sum.21
  1.2 0.1 copy.24
  1.2 0.1 fusion.1
  1.3 0.7 copy.25
  2.7 0.3 fusion
  3.0 0.7 pad_maximum_fusion
  3.8 85.3 %mixer.1 = (bf16[16,4096]{1,0:T(8,128)(2,1)}, bf16[8,8,4096]{2,1,0:T(8,128)(2,1)}) custom-call(bf16[128,4096]{1,0:T(8,128)(2,1)} %hidden.1, bf16[4096]{0:T(1024)(128)(2,1)} %attn_gain.1, bf16[256,512]{1,0:T(8,128)(2,1)} %w_query.1, bf16[256,128]{1,0:T(8,128)(2,1)} %w_key.1, bf16[256,128]{1,0:T(8,128)(2,1)} %w_value.1, bf16[512,256]{1,0:T(8,128)(2,1)} %w_out.1, ...), custom_call_target="tpu_custom_call" | custom-call | tf_op jit(solution)/shard_map/mixer/pallas_call | solution.py:665
  89.1 1.4 select_reduce_fusion.mix
  90.4 94.8 %experts.1 = bf16[16,4096]{1,0:T(8,128)(2,1)} custom-call(bf16[64,4096]{1,0:T(8,128)(2,1)} %bitcast.4, bf16[1,4096,896]{2,1,0:T(8,128)(2,1)} %gate.1, bf16[1,4096,896]{2,1,0:T(8,128)(2,1)} %up.1, bf16[1,896,4096]{2,1,0:T(8,128)(2,1)} %down.1, bf16[16,4096]{1,0:T(8,128)(2,1)} %get-tuple-element.8.residual, f32[16,64]{1,0:T(8,128)} %select_reduce_fusion.mix), custom_call_target="tpu_custom_call" | custom-call | tf_op jit(solution)/shard_map/experts/pallas_call | solution.py:381
  185.3 1.6 copy.29
  (4 shorter events, 0.0 us)
Async XLA Ops:
  0.0 0.7 copy-start

commit v5 on v4

--- a/solution.py
+++ b/solution.py
@@ -228,7 +228,7 @@
         )
 
     mine = pl.ds(0, ROWS)
-    lhs, rhs = pl.ds(0, half_width), pl.ds(half_width, half_width)
+    lhs, rhs = pl.ds(0, x_first.shape[-1]), pl.ds(x_first.shape[-1], x_sum.shape[-1])
 
     def to_sib(g):
         return rs_copy(g, part.at[g, pl.ds(ROWS, ROWS), :], from_sib.at[g], (0, 0, 1))
@@ -317,7 +317,7 @@
 
     def give_back(h, value):
         cols = rhs if h else lhs
-        slots[:, :, cols] = value.reshape(8, ROWS // 8, half_width).astype(bf16)
+        slots[:, :, cols] = value.reshape(8, ROWS // 8, -1).astype(bf16)
         moves[h] = [
             pltpu.make_async_remote_copy(
                 src_ref=slots.at[to, :, cols],
@@ -358,7 +358,7 @@
     for h, cols in ((1, rhs), (0, lhs)):
         for move in moves[h]:
             move.wait_recv()
-        outcome = returned[:, :, cols].astype(f32).reshape(ROWS, half_width).astype(bf16)
+        outcome = returned[:, :, cols].astype(f32).reshape(ROWS, -1).astype(bf16)
         mixture = jnp.dot(hi, outcome, preferred_element_type=f32) + jnp.dot(lo, outcome, preferred_element_type=f32)
         out[:, cols] = (residual[:, cols].astype(f32) + mixture).astype(bf16)
     for h in range(2):
@@ -377,6 +377,7 @@
 def experts(arrived, w_gate, w_up, w_down, residual, mix):
     rows, width = arrived.shape
     ff = w_gate.shape[2]
+    left = width * 5 // 8
     bf16 = jnp.bfloat16
     return pl.pallas_call(
         expert_kernel,
@@ -390,10 +391,10 @@
             pltpu.VMEM((2 * rows, ff), bf16),
             pltpu.VMEM((8, 2 * rows, width), bf16),
             pltpu.VMEM((8, rows, width), bf16),
-            pltpu.VMEM((3, 2, rows, width // 2), bf16),
-            pltpu.VMEM((rows, width // 2), bf16),
-            pltpu.VMEM((4, rows, width // 2), bf16),
-            pltpu.VMEM((3, rows, width // 2), bf16),
+            pltpu.VMEM((3, 2, rows, left), bf16),
+            pltpu.VMEM((rows, left), bf16),
+            pltpu.VMEM((4, rows, width - left), bf16),
+            pltpu.VMEM((3, rows, width - left), bf16),
             pltpu.VMEM((8, rows // 8, width), bf16),
             pltpu.VMEM((8, rows // 8, width), bf16),
             pltpu.SemaphoreType.DMA((len(PIECES), N_TRANSFERS)),
@@ -735,9 +736,11 @@
     earlier = jnp.arange(2 * tok_dev)[:, None] < jnp.arange(2 * tok_dev)[None, :]
     place = flat * capacity + jnp.sum(same & earlier, axis=0, dtype=jnp.int32)
     place = place.reshape(tok_dev, 2)
-    held = place[:, :, None] == jnp.arange(exp_count * capacity, dtype=jnp.int32)[None, None, :]
-    select = jnp.any(held, axis=1).T.astype(jnp.bfloat16)
-    mix = jnp.sum(jnp.where(held, gate_weights[:, :, None], 0.0), axis=1)
+    slot = jnp.arange(exp_count * capacity, dtype=jnp.int32)
+    select = ((slot[:, None] == place[None, :, 0]) | (slot[:, None] == place[None, :, 1])).astype(jnp.bfloat16)
+    mix = jnp.where(place[:, :1] == slot[None, :], gate_weights[:, :1], 0.0) + jnp.where(
+        place[:, 1:] == slot[None, :], gate_weights[:, 1:], 0.0
+    )
     residual, arrived = mixer(
         hidden_in,
         attn_gain,

time: 188 us -> 186 us (0.989)
  Pallas kernels: 180 us -> 178 us
where the time goes in v5:
time: 186 us; the launch traced here: 185 us
  Pallas kernels  178 us (96%)
  local copies, waits for them, and re-layouts  3.55 us (2%)
  other arithmetic  2.46 us (1%)
    pallas_call x1, Pallas kernels, experts(): pl.pallas_call(expert_kernel, out_shape=jax.ShapeDtypeStruct(residual.sha...  93.1 us
    pallas_call x1, Pallas kernels, mixer(): pl.pallas_call(mixer_kernel, out_shape=[jax.ShapeDtypeStruct((tokens // 8...  85.3 us

profile of v5, /device:TPU:1, one launch (start us, length us, event | category | flops | bytes accessed | tf_op | source)
XLA Modules:
  0.0 185.1 jit_solution(8309087561738764646)
XLA Ops:
  0.0 0.0 copy-start
  0.0 0.7 copy-done
  0.7 0.1 constant_dynamic-slice_fusion
  0.8 0.1 copy.19
  0.9 0.1 eq.72
  1.0 0.1 convert_reduce_fusion
  1.1 0.1 reduce_sum.12
  1.2 0.2 slice_reduce_fusion.1
  1.3 0.6 fusion.1.select
  2.6 0.3 fusion.2
  3.0 0.7 pad_maximum_fusion
  3.7 85.3 %mixer.1 = (bf16[16,4096]{1,0:T(8,128)(2,1)}, bf16[8,8,4096]{2,1,0:T(8,128)(2,1)}) custom-call(bf16[128,4096]{1,0:T(8,128)(2,1)} %hidden.1, bf16[4096]{0:T(1024)(128)(2,1)} %attn_gain.1, bf16[256,512]{1,0:T(8,128)(2,1)} %w_query.1, bf16[256,128]{1,0:T(8,128)(2,1)} %w_key.1, bf16[256,128]{1,0:T(8,128)(2,1)} %w_value.1, bf16[512,256]{1,0:T(8,128)(2,1)} %w_out.1, ...), custom_call_target="tpu_custom_call" | custom-call | tf_op jit(solution)/shard_map/mixer/pallas_call | solution.py:666
  89.0 0.8 slice_bitcast_fusion.1
  89.7 0.7 select_add_fusion.mix
  90.4 93.1 %experts.1 = bf16[16,4096]{1,0:T(8,128)(2,1)} custom-call(bf16[64,4096]{1,0:T(8,128)(2,1)} %bitcast.7, bf16[1,4096,896]{2,1,0:T(8,128)(2,1)} %gate.1, bf16[1,4096,896]{2,1,0:T(8,128)(2,1)} %up.1, bf16[1,896,4096]{2,1,0:T(8,128)(2,1)} %down.1, bf16[16,4096]{1,0:T(8,128)(2,1)} %get-tuple-element.8.residual, f32[16,64]{1,0:T(8,128)} %select_add_fusion.mix), custom_call_target="tpu_custom_call" | custom-call | tf_op jit(solution)/shard_map/experts/pallas_call | solution.py:382
  183.6 1.6 copy.22
  (3 shorter events, 0.0 us)
Async XLA Ops:
  0.0 0.7 copy-start

commit v6 on v5

--- a/solution.py
+++ b/solution.py
@@ -154,7 +154,7 @@
 CHIPS = ((0, 0), (0, 1), (3, 0), (1, 0), (3, 1), (1, 1), (2, 1), (2, 0))
 SOURCE = {1: 0, 3: 1, 2: 2}
 ROWS = 64
-PIECES = ((X_THEN_Y, 16), (Y_THEN_X, 48))
+PIECES = ((Y_THEN_X, 48), (X_THEN_Y, 16))
 
 
 class LocalGather(Gather):

time: 186 us -> 186 us (level)
  no operation moved by 1% of the time
where the time goes in v6:
time: 186 us; the launch traced here: 185 us
  Pallas kernels  178 us (96%)
  local copies, waits for them, and re-layouts  3.55 us (2%)
  other arithmetic  2.46 us (1%)
    pallas_call x1, Pallas kernels, experts(): pl.pallas_call(expert_kernel, out_shape=jax.ShapeDtypeStruct(residual.sha...  93.1 us
    pallas_call x1, Pallas kernels, mixer(): pl.pallas_call(mixer_kernel, out_shape=[jax.ShapeDtypeStruct((tokens // 8...  85.3 us

profile of v6, /device:TPU:1, one launch (start us, length us, event | category | flops | bytes accessed | tf_op | source)
XLA Modules:
  0.0 185.1 jit_solution(13291746806222488010)
XLA Ops:
  0.0 0.0 copy-start
  0.0 0.7 copy-done
  0.7 0.1 constant_dynamic-slice_fusion
  0.8 0.1 copy.19
  0.9 0.1 eq.72
  1.0 0.1 convert_reduce_fusion
  1.1 0.1 reduce_sum.12
  1.2 0.2 slice_reduce_fusion.1
  1.3 0.6 fusion.1.select
  2.6 0.3 fusion.2
  3.0 0.7 pad_maximum_fusion
  3.7 85.3 %mixer.1 = (bf16[16,4096]{1,0:T(8,128)(2,1)}, bf16[8,8,4096]{2,1,0:T(8,128)(2,1)}) custom-call(bf16[128,4096]{1,0:T(8,128)(2,1)} %hidden.1, bf16[4096]{0:T(1024)(128)(2,1)} %attn_gain.1, bf16[256,512]{1,0:T(8,128)(2,1)} %w_query.1, bf16[256,128]{1,0:T(8,128)(2,1)} %w_key.1, bf16[256,128]{1,0:T(8,128)(2,1)} %w_value.1, bf16[512,256]{1,0:T(8,128)(2,1)} %w_out.1, ...), custom_call_target="tpu_custom_call" | custom-call | tf_op jit(solution)/shard_map/mixer/pallas_call | solution.py:666
  89.0 0.8 slice_bitcast_fusion.1
  89.7 0.7 select_add_fusion.mix
  90.4 93.1 %experts.1 = bf16[16,4096]{1,0:T(8,128)(2,1)} custom-call(bf16[64,4096]{1,0:T(8,128)(2,1)} %bitcast.7, bf16[1,4096,896]{2,1,0:T(8,128)(2,1)} %gate.1, bf16[1,4096,896]{2,1,0:T(8,128)(2,1)} %up.1, bf16[1,896,4096]{2,1,0:T(8,128)(2,1)} %down.1, bf16[16,4096]{1,0:T(8,128)(2,1)} %get-tuple-element.8.residual, f32[16,64]{1,0:T(8,128)} %select_add_fusion.mix), custom_call_target="tpu_custom_call" | custom-call | tf_op jit(solution)/shard_map/experts/pallas_call | solution.py:382
  183.6 1.6 copy.22
  (3 shorter events, 0.0 us)
Async XLA Ops:
  0.0 0.7 copy-start
